TPU v7x, 32 devices: a whole 2x2x4 slice. The times are simulated.
32 devices in a mesh: grp: 2 (over y), chol: 4 (over z), orb: 4 (over x, core).
Axes of the slice: x: 2, y: 2, z: 4, core: 2. Of those that a mesh axis runs over, the one named last changes fastest.
Arguments:
- green: bfloat16 [32, 600, 896], P(('grp', 'chol'), None, 'orb'), parts along dimension 0, may hold values from -6 to 6
- half_chol: bfloat16 [80, 600, 896], P(('grp', 'chol'), None, 'orb'), parts along dimension 0, may hold values from -0.0078125 to 0.0078125
- chol_vec: bfloat16 [80, 896, 896], P(('grp', 'chol'), 'orb'), parts along dimension 0, may hold values from -0.0546875 to 0.0546875
- noise: float32 [32, 40], P('grp', 'chol'), parts along dimension 0, may hold values from -6 to 6
- order: int32 [32], P('grp'), parts along dimension 0, may hold values from 0 to 15, each once
- walkers: bfloat16 [32, 600, 896], P(('grp', 'chol'), None, 'orb'), parts along dimension 0, may hold values from -3 to 3
Outputs:
- force_bias: float32 [32, 40], P('grp', 'chol'), parts along dimension 0
- propagated: bfloat16 [32, 600, 896], P(('grp', 'chol'), None, 'orb'), parts along dimension 0
There are 2 independent parts, one for each index of `grp`. A program takes and returns all parts, laid end to end along the dimension named above; each array names one. Nothing has to cross between parts.
Inputs may be any that keep to these rules, and one draw needn't show every extreme that they name: order is a permutation of the 16 walkers.
All inputs are finite; a program needn't handle non-finite values.
Results may differ from a plain program's by a relative error of at most 0.0086.
Values may be sent and summed in bfloat16 or wider, within the bound.
A program may use at most 64 MiB of HBM per device.

v0:
```python
import jax
import jax.numpy as jnp
from jax import lax
from jax.experimental import pallas as pl
from jax.experimental.pallas import tpu as pltpu
from jax.sharding import PartitionSpec as P

TERMS = 6


def ring(n):
    return [(i, (i + 1) % n) for i in range(n)]


def force_of(green, half_chol):
    n = lax.axis_size("chol")
    me = lax.axis_index("chol")
    each = green.shape[0]
    values = jnp.zeros((n * each, half_chol.shape[0]), jnp.float32)
    block = green
    for step in range(n):
        later = lax.ppermute(block, "chol", ring(n)) if step < n - 1 else None
        part = jnp.einsum("wiq,giq->wg", block, half_chol, preferred_element_type=jnp.float32)
        owner = lax.rem(me - step + n, n)
        values = lax.dynamic_update_slice(values, part, (owner * each, 0))
        block = later
    return values


def summed_rows(fields, chol_vec, each, chunks):
    n = lax.axis_size("chol")
    me = lax.axis_index("chol")
    size = each // chunks
    done = [None] * chunks
    for step in range(n):
        owner = lax.rem(me - step - 1 + 2 * n, n)
        for c in range(chunks):
            mine = lax.dynamic_slice(
                fields, (owner * each + c * size, 0), (size, fields.shape[1])
            )
            part = jnp.einsum("wg,gpq->wpq", mine, chol_vec, preferred_element_type=jnp.float32)
            if done[c] is not None:
                part = part + done[c].astype(jnp.float32)
            part = part.astype(jnp.bfloat16)
            done[c] = lax.ppermute(part, "chol", ring(n)) if step < n - 1 else part
    return done


def rows_of(fields, chol_vec, start, size):
    mine = lax.dynamic_slice(fields, (start, 0), (size, fields.shape[1]))
    return jnp.einsum("wg,gpq->wpq", mine, chol_vec, preferred_element_type=jnp.float32)


def line_of_four(green, half_chol, chol_vec, noise, order, each, chunks):
    me = lax.axis_index("chol")
    inner = jnp.logical_and(me >= 1, me <= 2)

    def go(array, pairs):
        return lax.ppermute(array, "chol", pairs)

    r1 = go(green, [(0, 1), (1, 2), (2, 3)])
    l1 = go(green, [(1, 0), (2, 1), (3, 2)])
    r2 = go(r1, [(1, 2), (2, 3)])
    l2 = go(l1, [(2, 1), (1, 0)])
    r3 = go(r2, [(2, 3)])
    l3 = go(l2, [(1, 0)])
    high = chol_vec.shape[1] // chunks
    own_chol, far_chol = [], []
    after = (r1, l1)
    for c in range(chunks):
        part = chol_vec[:, c * high : (c + 1) * high]
        own_chol.append(part)
        held_back = lax.optimization_barrier((part,) + after)[0]
        got = go(held_back, [(0, 1), (3, 2)])
        far_chol.append(got)
        after = (got,)

    values = jnp.zeros((4 * each, half_chol.shape[0]), jnp.float32)
    for block, owner in (
        (green, me),
        (l1 + r3, (me + 1) % 4),
        (r2 + l2, (me + 2) % 4),
        (r1 + l3, (me + 3) % 4),
    ):
        part = jnp.einsum("wiq,giq->wg", block, half_chol, preferred_element_type=jnp.float32)
        values = lax.dynamic_update_slice(values, part, (owner * each, 0))
    values = lax.psum(values, "orb")
    force_bias = jnp.take(values, order, axis=0)
    fields = (noise - force_bias).astype(jnp.bfloat16)
    end_fields = go(fields, [(0, 1), (3, 2)])

    near = jnp.where(me <= 1, 0, 3) * each
    far = jnp.where(me <= 1, 3, 0) * each
    across = jnp.where(me <= 1, 2, 1) * each
    rows = []
    for c in range(chunks):
        def share(start):
            return rows_of(fields, own_chol[c], start, each) + rows_of(
                end_fields, far_chol[c], start, each
            )

        first = go(share(far).astype(jnp.bfloat16), [(1, 2), (2, 1)])
        second = go(share(across).astype(jnp.bfloat16), [(1, 2), (2, 1)])
        ends = (first.astype(jnp.float32) + share(near)).astype(jnp.bfloat16)
        ends = go(ends, [(1, 0), (2, 3)])
        own = (second.astype(jnp.float32) + share(me * each)).astype(jnp.bfloat16)
        rows.append(jnp.where(inner, own, ends))
    return force_bias, rows


def taylor_kernel(held_ref, prop_ref, out_ref, term, running):
    parts, _, wide = held_ref.shape
    for j in range(parts):
        cols = slice(j * wide, (j + 1) * wide)
        term[0, :, cols] = held_ref[j]
        running[:, cols] = held_ref[j].astype(jnp.float32)
    total = parts * wide

    def step(now, later, factor):
        for low in range(0, total, 256):
            cols = slice(low, min(low + 256, total))
            scaled = (
                lax.dot_general(
                    term[now],
                    prop_ref[cols, :],
                    (((1,), (1,)), ((), ())),
                    preferred_element_type=jnp.float32,
                )
                * factor
            )
            running[:, cols] += scaled
            term[later, :, cols] = scaled.astype(jnp.bfloat16)

    for power in range(1, TERMS + 1):
        step((power - 1) % 2, power % 2, 1.0 / power)
    for j in range(parts):
        out_ref[j] = running[:, j * wide : (j + 1) * wide].astype(out_ref.dtype)


def taylor(held, prop):
    parts, tall, wide = held.shape
    return pl.pallas_call(
        taylor_kernel,
        out_shape=jax.ShapeDtypeStruct(held.shape, held.dtype),
        in_specs=[pl.BlockSpec(memory_space=pltpu.VMEM)] * 2,
        out_specs=pl.BlockSpec(memory_space=pltpu.VMEM),
        scratch_shapes=[
            pltpu.VMEM((2, tall, parts * wide), jnp.bfloat16),
            pltpu.VMEM((tall, parts * wide), jnp.float32),
        ],
        compiler_params=pltpu.CompilerParams(vmem_limit_bytes=40 * 2**20),
        cost_estimate=pl.CostEstimate(
            flops=2 * TERMS * tall * (parts * wide) ** 2,
            bytes_accessed=6 * tall * parts * wide,
            transcendentals=0,
        ),
    )(held, prop)


def body(green, half_chol, chol_vec, noise, order, walkers):
    each = walkers.shape[0]
    orb = lax.axis_size("orb")
    whole = each == orb
    if whole:
        held = lax.all_to_all(walkers, "orb", split_axis=0, concat_axis=0, tiled=True)
    else:
        held = lax.all_to_all(walkers, "orb", split_axis=1, concat_axis=2, tiled=True)

    if lax.axis_size("chol") == 4:
        force_bias, rows = line_of_four(
            green, half_chol, chol_vec, noise, order, each, 2 if whole else 1
        )
    else:
        values = lax.psum(force_of(green, half_chol), "orb")
        force_bias = jnp.take(values, order, axis=0)
        fields = (noise - force_bias).astype(jnp.bfloat16)
        chunks = 2 if each % 2 == 0 else 1
        rows = [jnp.concatenate(summed_rows(fields, chol_vec, each, chunks), axis=0)]
    if whole:
        arrived = [
            lax.all_to_all(part, "orb", split_axis=0, concat_axis=0, tiled=True) for part in rows
        ]
        prop = jnp.concatenate(arrived, axis=1)
        prop = prop.reshape(-1, prop.shape[2])
        blocks = taylor(held, prop)
        propagated = lax.all_to_all(blocks, "orb", split_axis=0, concat_axis=0, tiled=True)
        return (force_bias, propagated)
    prop = lax.all_gather(jnp.concatenate(rows, axis=1), "orb", axis=1, tiled=True)
    running = held.astype(jnp.float32)
    term_now = held
    for power in range(1, TERMS + 1):
        scaled = (
            jnp.einsum("wiq,wpq->wip", term_now, prop, preferred_element_type=jnp.float32)
            / power
        )
        running = running + scaled
        term_now = scaled.astype(jnp.bfloat16)
    propagated = lax.all_to_all(
        running.astype(jnp.bfloat16), "orb", split_axis=2, concat_axis=1, tiled=True
    )
    return (force_bias, propagated)


def solution(mesh):
    return jax.shard_map(
        body,
        mesh=mesh,
        in_specs=(
            P(("grp", "chol"), None, "orb"),
            P(("grp", "chol"), None, "orb"),
            P(("grp", "chol"), "orb", None),
            P("grp", "chol"),
            P("grp"),
            P(("grp", "chol"), None, "orb"),
        ),
        out_specs=(P("grp", "chol"), P(("grp", "chol"), None, "orb")),
        check_vma=False,
    )
```

profile of v0, /device:TPU:8, one launch (start us, length us, event | category | flops | bytes accessed | tf_op | source)
XLA Modules:
  0.0 268.7 jit_solution(13418694252726464958)
XLA Ops:
  0.6 3.8 %collective-permute-start.1 = (bf16[4,600,224]{1,2,0:T(8,128)(2,1)}, bf16[4,600,224]{1,2,0:T(8,128)(2,1)S(1)}, u32[]{:S(2)}, u32[]{:S(2)}) collective-permute-start(bf16[4,600,224]{1,2,0:T(8,128)(2,1)} %param.6), channel_id=1, source_target_pairs={{0,4},{4,8},{8,12},{1,5},{5,9},{9,13},{2,6},{6,10},{10,14},{3,7},{... | collective-permute-start | bytes 3225608 | tf_op jit(solution)/shard_map/ppermute | solution.py:59
  4.4 2.4 collective-permute-start
  6.8 23.2 %collective-permute-done.1 = bf16[4,600,224]{1,2,0:T(8,128)(2,1)S(1)} collective-permute-done((bf16[4,600,224]{1,2,0:T(8,128)(2,1)}, bf16[4,600,224]{1,2,0:T(8,128)(2,1)S(1)}, u32[]{:S(2)}, u32[]{:S(2)}) %collective-permute-start.1) | collective-permute-done | bytes 1075232 | tf_op jit(solution)/shard_map/ppermute | solution.py:59
  30.0 4.5 %collective-permute-start.2 = (bf16[4,600,224]{1,2,0:T(8,128)(2,1)S(1)}, bf16[4,600,224]{1,2,0:T(8,128)(2,1)}, u32[]{:S(2)}, u32[]{:S(2)}) collective-permute-start(bf16[4,600,224]{1,2,0:T(8,128)(2,1)S(1)} %collective-permute-done.1), channel_id=1, source_target_pairs={{4,8},{8,12},{5,9},{9,13},{6,10},{10,14},{7,11},{11,15},{20,24},{2... | collective-permute-start | bytes 3225608 | tf_op jit(solution)/shard_map/ppermute | solution.py:59
  34.5 3.8 %fusion.130 = (bf16[10,112,896]{2,1,0:T(8,128)(2,1)S(1)}, bf16[10,112,896]{2,1,0:T(8,128)(2,1)}) fusion(bf16[10,224,896]{2,1,0:T(8,128)(2,1)} %param.8), kind=kLoop, calls=%fused_computation.85 | loop fusion | bytes 8028160 | tf_op jit(solution)/shard_map/slice | solution.py:71
  39.7 1.7 copy.30
  42.6 5.8 %collective-permute-start.4 = (bf16[4,600,224]{1,2,0:T(8,128)(2,1)}, bf16[4,600,224]{1,2,0:T(8,128)(2,1)}, u32[]{:S(2)}, u32[]{:S(2)}) collective-permute-start(bf16[4,600,224]{1,2,0:T(8,128)(2,1)} %collective-permute-done), channel_id=1, source_target_pairs={{8,4},{4,0},{9,5},{5,1},{10,6},{6,2},{11,7},{7,3},{24,20},{20,16},... | collective-permute-start | bytes 3225608 | tf_op jit(solution)/shard_map/ppermute | solution.py:59
  48.5 8.7 %collective-permute-done.2 = bf16[4,600,224]{1,2,0:T(8,128)(2,1)} collective-permute-done((bf16[4,600,224]{1,2,0:T(8,128)(2,1)S(1)}, bf16[4,600,224]{1,2,0:T(8,128)(2,1)}, u32[]{:S(2)}, u32[]{:S(2)}) %collective-permute-start.2) | collective-permute-done | bytes 1075232 | tf_op jit(solution)/shard_map/ppermute | solution.py:59
  57.2 1.7 collective-permute-start.3
  58.9 4.3 %all-to-all-start = ((bf16[4,600,224]{1,2,0:T(8,128)(2,1)}), bf16[4,600,224]{1,2,0:T(8,128)(2,1)}, u32[]{:S(2)}, u32[]{:S(2)}) async-start(bf16[4,600,224]{1,2,0:T(8,128)(2,1)} %param.11), calls=%async_computation | async-start | bytes 2293760 | tf_op jit(solution)/shard_map/all_to_all | solution.py:165
  63.2 3.8 %copy.46 = bf16[10,112,896]{2,0,1:T(8,128)(2,1)} copy(bf16[10,112,896]{2,1,0:T(8,128)(2,1)} %get-tuple-element.11) | data formatting | bytes 4014080 | tf_op jit(solution)/shard_map/optimization_barrier | solution.py:73
  67.1 3.3 %fusion.49 = f32[16,10]{1,0:T(8,128)S(1)} fusion(f32[16,10]{1,0:T(8,128)S(1)} %broadcast_in_dim.16, s32[]{:T(128)S(6)} %select_n.81, bf16[10,600,224]{1,2,0:T(8,128)(2,1)S(1)} %copy-done, bf16[4,600,224]{1,2,0:T(8,128)(2,1)} %param.6), kind=kOutput, calls=%fused_computation.39 | convolution fusion | flops 10752000 | bytes 3944452 | tf_op jit(solution)/shard_map/wiq,giq->wg/dot_general | solution.py:85
  70.4 1.6 collective-permute-done.4
  72.0 4.4 %collective-permute-start.5 = (bf16[4,600,224]{1,2,0:T(8,128)(2,1)}, bf16[4,600,224]{1,2,0:T(8,128)(2,1)S(1)}, u32[]{:S(2)}, u32[]{:S(2)}) collective-permute-start(bf16[4,600,224]{1,2,0:T(8,128)(2,1)} %collective-permute-done.4), channel_id=1, source_target_pairs={{4,0},{5,1},{6,2},{7,3},{20,16},{21,17},{22,18},{23,19}} | collective-permute-start | bytes 3225608 | tf_op jit(solution)/shard_map/ppermute | solution.py:59
  76.5 1.9 add.110
  78.4 9.6 %collective-permute-done.7 = bf16[10,112,896]{2,1,0:T(8,128)(2,1)} collective-permute-done((bf16[10,112,896]{2,1,0:T(8,128)(2,1)}, bf16[10,112,896]{2,1,0:T(8,128)(2,1)}, u32[]{:S(2)}, u32[]{:S(2)}) %collective-permute-start.7) | collective-permute-done | bytes 2007072 | tf_op jit(solution)/shard_map/ppermute | solution.py:59
  88.0 1.7 copy.37
  90.9 1.9 add.106
  92.8 2.0 fusion.59
  94.8 2.0 fusion.69
  96.9 2.1 collective-permute-done.5
  99.3 2.0 fusion.79
  101.3 6.2 %psum.7 = f32[16,10]{1,0:T(8,128)S(1)} all-reduce(f32[16,10]{1,0:T(8,128)S(1)} %fusion.79), channel_id=1, replica_groups=mesh['grp'=2,'chol'=4,'orb'=4] {'orb'}, use_global_device_ids=true, to_apply=%region_0.1 | all-reduce | flops 160 | bytes 1280 | tf_op jit(solution)/shard_map/psum | solution.py:87
  108.7 1.6 collective-permute-start.6
  110.3 2.2 fusion.96
  116.0 19.4 %collective-permute-done.6 = bf16[16,10]{1,0:T(8,128)(2,1)S(1)} collective-permute-done((bf16[16,10]{1,0:T(8,128)(2,1)S(1)}, bf16[16,10]{1,0:T(8,128)(2,1)S(1)}, u32[]{:S(2)}, u32[]{:S(2)}) %collective-permute-start.6) | collective-permute-done | bytes 352 | tf_op jit(solution)/shard_map/ppermute | solution.py:59
  135.3 2.3 add_convert_fusion.5
  137.7 2.3 collective-permute-start.9
  140.6 2.3 add_convert_fusion.7
  142.9 3.6 %collective-permute-start.8 = (bf16[4,112,896]{2,0,1:T(4,128)(2,1)S(1)}, bf16[4,112,896]{2,0,1:T(4,128)(2,1)S(1)}, u32[]{:S(2)}, u32[]{:S(2)}) collective-permute-start(bf16[4,112,896]{2,0,1:T(4,128)(2,1)S(1)} %add_convert_fusion.7), channel_id=1, source_target_pairs={{4,8},{8,4},{5,9},{9,5},{6,10},{10,6},{7,11},{11,7},{20,24},{24,20... | collective-permute-start | bytes 2408456 | tf_op jit(solution)/shard_map/ppermute | solution.py:59
  146.5 2.3 add_convert_fusion.1
  148.8 2.3 collective-permute-start.13
  151.1 9.3 %collective-permute-done.9 = bf16[4,112,896]{2,0,1:T(4,128)(2,1)S(1)} collective-permute-done((bf16[4,112,896]{2,0,1:T(4,128)(2,1)S(1)}, bf16[4,112,896]{2,0,1:T(4,128)(2,1)S(1)}, u32[]{:S(2)}, u32[]{:S(2)}) %collective-permute-start.9) | collective-permute-done | bytes 802848 | tf_op jit(solution)/shard_map/ppermute | solution.py:59
  160.4 2.5 add_convert_fusion.4
  164.9 3.3 %add_convert_fusion.3 = bf16[4,112,896]{2,0,1:T(4,128)(2,1)} fusion(f32[4,112,896]{2,0,1:T(4,128)S(1)} %fusion.90, bf16[10,112,896]{2,1,0:T(8,128)(2,1)} %collective-permute-done.11, bf16[16,10]{1,0:T(8,128)(2,1)S(1)} %collective-permute-done.6, s32[]{:T(128)S(6)} %select_n.91), kind=kOutput, calls=%fused_computation.29 | convolution fusion | flops 8830976 | bytes 4416516 | tf_op jit(solution)/shard_map/wg,gpq->wpq/dot_general | solution.py:51
  168.2 2.3 collective-permute-start.12
  170.4 24.4 %collective-permute-done.13 = bf16[4,112,896]{2,0,1:T(4,128)(2,1)S(1)} collective-permute-done((bf16[4,112,896]{2,0,1:T(4,128)(2,1)S(1)}, bf16[4,112,896]{2,0,1:T(4,128)(2,1)S(1)}, u32[]{:S(2)}, u32[]{:S(2)}) %collective-permute-start.13) | collective-permute-done | bytes 802848 | tf_op jit(solution)/shard_map/ppermute | solution.py:59
  194.8 3.4 %add_convert_fusion = bf16[4,112,896]{2,0,1:T(4,128)(2,1)} fusion(f32[4,112,896]{2,0,1:T(4,128)S(1)} %fusion.84, bf16[4,112,896]{2,0,1:T(4,128)(2,1)S(1)} %collective-permute-done.13, bf16[10,112,896]{2,1,0:T(8,128)(2,1)} %collective-permute-done.11, bf16[16,10]{1,0:T(8,128)(2,1)S(1)} %collective-permute-done.6, s32[]{:T(128)S(6)} %select_n.95), kind=kOutput, calls=%fused_computation.26 | convolution fusion | flops 9633792 | bytes 5219332 | tf_op jit(solution)/shard_map/wg,gpq->wpq/dot_general | solution.py:51
  198.2 2.2 collective-permute-start.14
  200.4 2.7 fusion.100
  204.1 3.7 %all-to-all-start.1 = ((bf16[4,112,896]{2,1,0:T(8,128)(2,1)}), bf16[4,112,896]{2,1,0:T(8,128)(2,1)S(1)}, u32[]{:S(2)}, u32[]{:S(2)}) async-start(bf16[4,112,896]{2,1,0:T(8,128)(2,1)} %copy.35), calls=%async_computation.1 | async-start | bytes 1605632 | tf_op jit(solution)/shard_map/all_to_all | solution.py:181
  209.5 2.9 %fusion.103 = bf16[4,112,896]{2,0,1:T(4,128)(2,1)S(1)} fusion(bf16[4,112,896]{2,0,1:T(4,128)(2,1)} %collective-permute-done.14, f32[4,112,896]{2,0,1:T(4,128)S(1)} %fusion.88, bf16[10,112,896]{2,1,0:T(8,128)(2,1)} %collective-permute-done.11, bf16[4,112,896]{2,0,1:T(4,128)(2,1)} %collective-permute-done.12, pred[]{:T(512)S(6)} %and.26, ...), kind=kOutput, calls=%fused_computation.63 | convolution fusion | flops 10035200 | bytes 6022149 | tf_op jit(solution)/shard_map/wg,gpq->wpq/dot_general | solution.py:51
  213.4 6.0 %all-to-all-done.1 = bf16[4,112,896]{2,1,0:T(8,128)(2,1)S(1)} async-done(((bf16[4,112,896]{2,1,0:T(8,128)(2,1)}), bf16[4,112,896]{2,1,0:T(8,128)(2,1)S(1)}, u32[]{:S(2)}, u32[]{:S(2)}) %all-to-all-start.1) | async-done | bytes 802848 | tf_op jit(solution)/shard_map/all_to_all | solution.py:181
  219.4 4.2 %all-to-all-start.2 = ((bf16[4,112,896]{2,1,0:T(8,128)(2,1)}), bf16[4,112,896]{2,1,0:T(8,128)(2,1)}, u32[]{:S(2)}, u32[]{:S(2)}) async-start(bf16[4,112,896]{2,1,0:T(8,128)(2,1)} %copy.42), calls=%async_computation.2 | async-start | bytes 1605632 | tf_op jit(solution)/shard_map/all_to_all | solution.py:181
  225.2 10.3 %all-to-all-done.2 = bf16[4,112,896]{2,1,0:T(8,128)(2,1)} async-done(((bf16[4,112,896]{2,1,0:T(8,128)(2,1)}), bf16[4,112,896]{2,1,0:T(8,128)(2,1)}, u32[]{:S(2)}, u32[]{:S(2)}) %all-to-all-start.2) | async-done | bytes 802848 | tf_op jit(solution)/shard_map/all_to_all | solution.py:181
  237.0 8.1 %shard_map.77 = bf16[4,600,224]{2,1,0:T(8,128)(2,1)S(1)} custom-call(bf16[4,600,224]{2,1,0:T(8,128)(2,1)S(1)} %copy.43.held_ref, bf16[896,896]{1,0:T(8,128)(2,1)S(1)} %bitcast.49), custom_call_target="tpu_custom_call" | custom-call | flops 5780275200 | bytes 3225600 | tf_op jit(solution)/shard_map/pallas_call | solution.py:142
  246.1 2.5 copy.44
  248.7 19.0 %all_to_all.20 = bf16[4,600,224]{1,2,0:T(8,128)(2,1)S(1)} all-to-all(bf16[4,600,224]{1,2,0:T(8,128)(2,1)} %copy.44), channel_id=1, replica_groups=mesh['grp'=2,'chol'=4,'orb'=4] {'orb'}, dimensions={0} | all-to-all | bytes 2150400 | tf_op jit(solution)/shard_map/all_to_all | solution.py:186
  (55 shorter events, 20.4 us)
Async XLA Ops:
  0.6 66.4 %copy-start = (bf16[10,600,224]{1,2,0:T(8,128)(2,1)S(1)}, bf16[10,600,224]{1,2,0:T(8,128)(2,1)}, u32[]{:S(2)}) copy-start(bf16[10,600,224]{1,2,0:T(8,128)(2,1)} %param.7) | copy-start | bytes 8064004
  0.6 29.4 %collective-permute-start.1 = (bf16[4,600,224]{1,2,0:T(8,128)(2,1)}, bf16[4,600,224]{1,2,0:T(8,128)(2,1)S(1)}, u32[]{:S(2)}, u32[]{:S(2)}) collective-permute-start(bf16[4,600,224]{1,2,0:T(8,128)(2,1)} %param.6), channel_id=1, source_target_pairs={{0,4},{4,8},{8,12},{1,5},{5,9},{9,13},{2,6},{6,10},{10,14},{3,7},{... | collective-permute-start | bytes 3225608 | tf_op jit(solution)/shard_map/ppermute | solution.py:59
  4.4 35.3 %collective-permute-start = (bf16[4,600,224]{1,2,0:T(8,128)(2,1)}, bf16[4,600,224]{1,2,0:T(8,128)(2,1)}, u32[]{:S(2)}, u32[]{:S(2)}) collective-permute-start(bf16[4,600,224]{1,2,0:T(8,128)(2,1)} %param.6), channel_id=1, source_target_pairs={{4,0},{8,4},{12,8},{5,1},{9,5},{13,9},{6,2},{10,6},{14,10},{7,3},{... | collective-permute-start | bytes 3225608 | tf_op jit(solution)/shard_map/ppermute | solution.py:59
  30.0 8.3 %copy-start.8 = (bf16[4,600,224]{1,2,0:T(8,128)(2,1)}, bf16[4,600,224]{1,2,0:T(8,128)(2,1)S(1)}, u32[]{:S(2)}) copy-start(bf16[4,600,224]{1,2,0:T(8,128)(2,1)S(1)} %collective-permute-done.1) | copy-start | bytes 3225604
  30.0 27.2 %collective-permute-start.2 = (bf16[4,600,224]{1,2,0:T(8,128)(2,1)S(1)}, bf16[4,600,224]{1,2,0:T(8,128)(2,1)}, u32[]{:S(2)}, u32[]{:S(2)}) collective-permute-start(bf16[4,600,224]{1,2,0:T(8,128)(2,1)S(1)} %collective-permute-done.1), channel_id=1, source_target_pairs={{4,8},{8,12},{5,9},{9,13},{6,10},{10,14},{7,11},{11,15},{20,24},{2... | collective-permute-start | bytes 3225608 | tf_op jit(solution)/shard_map/ppermute | solution.py:59
  38.3 1.4 copy-start.4
  41.4 46.6 %collective-permute-start.7 = (bf16[10,112,896]{2,1,0:T(8,128)(2,1)}, bf16[10,112,896]{2,1,0:T(8,128)(2,1)}, u32[]{:S(2)}, u32[]{:S(2)}) collective-permute-start(bf16[10,112,896]{2,1,0:T(8,128)(2,1)} %copy.30), channel_id=1, source_target_pairs={{0,4},{12,8},{1,5},{13,9},{2,6},{14,10},{3,7},{15,11},{16,20},{28,... | collective-permute-start | bytes 6021128 | tf_op jit(solution)/shard_map/ppermute | solution.py:59
  42.6 29.3 %collective-permute-start.4 = (bf16[4,600,224]{1,2,0:T(8,128)(2,1)}, bf16[4,600,224]{1,2,0:T(8,128)(2,1)}, u32[]{:S(2)}, u32[]{:S(2)}) collective-permute-start(bf16[4,600,224]{1,2,0:T(8,128)(2,1)} %collective-permute-done), channel_id=1, source_target_pairs={{8,4},{4,0},{9,5},{5,1},{10,6},{6,2},{11,7},{7,3},{24,20},{20,16},... | collective-permute-start | bytes 3225608 | tf_op jit(solution)/shard_map/ppermute | solution.py:59
  57.2 33.7 %collective-permute-start.3 = (bf16[4,600,224]{1,2,0:T(8,128)(2,1)}, bf16[4,600,224]{1,2,0:T(8,128)(2,1)}, u32[]{:S(2)}, u32[]{:S(2)}) collective-permute-start(bf16[4,600,224]{1,2,0:T(8,128)(2,1)} %collective-permute-done.2), channel_id=1, source_target_pairs={{8,12},{9,13},{10,14},{11,15},{24,28},{25,29},{26,30},{27,31}} | collective-permute-start | bytes 3225608 | tf_op jit(solution)/shard_map/ppermute | solution.py:59
  58.9 145.2 %all-to-all-start = ((bf16[4,600,224]{1,2,0:T(8,128)(2,1)}), bf16[4,600,224]{1,2,0:T(8,128)(2,1)}, u32[]{:S(2)}, u32[]{:S(2)}) async-start(bf16[4,600,224]{1,2,0:T(8,128)(2,1)} %param.11), calls=%async_computation | async-start | bytes 2293760 | tf_op jit(solution)/shard_map/all_to_all | solution.py:165
  63.2 3.8 %copy-start.11 = (s32[16]{0:T(128)S(1)}, s32[16]{0:T(128)}, u32[]{:S(2)}) copy-start(s32[16]{0:T(128)} %param.10) | copy-start | bytes 196
  70.4 17.6 %copy-start.6 = (bf16[10,112,896]{2,0,1:T(8,128)(2,1)S(1)}, bf16[10,112,896]{2,0,1:T(8,128)(2,1)}, u32[]{:S(2)}) copy-start(bf16[10,112,896]{2,0,1:T(8,128)(2,1)} %copy.46) | copy-start | bytes 6021124
  72.0 27.0 %collective-permute-start.5 = (bf16[4,600,224]{1,2,0:T(8,128)(2,1)}, bf16[4,600,224]{1,2,0:T(8,128)(2,1)S(1)}, u32[]{:S(2)}, u32[]{:S(2)}) collective-permute-start(bf16[4,600,224]{1,2,0:T(8,128)(2,1)} %collective-permute-done.4), channel_id=1, source_target_pairs={{4,0},{5,1},{6,2},{7,3},{20,16},{21,17},{22,18},{23,19}} | collective-permute-start | bytes 3225608 | tf_op jit(solution)/shard_map/ppermute | solution.py:59
  89.6 56.9 %collective-permute-start.11 = (bf16[10,112,896]{2,1,0:T(8,128)(2,1)}, bf16[10,112,896]{2,1,0:T(8,128)(2,1)}, u32[]{:S(2)}, u32[]{:S(2)}) collective-permute-start(bf16[10,112,896]{2,1,0:T(8,128)(2,1)} %copy.37), channel_id=1, source_target_pairs={{0,4},{12,8},{1,5},{13,9},{2,6},{14,10},{3,7},{15,11},{16,20},{28,... | collective-permute-start | bytes 6021128 | tf_op jit(solution)/shard_map/ppermute | solution.py:59
  94.8 4.1 %copy-start.9 = (bf16[4,600,224]{1,2,0:T(8,128)(2,1)S(1)}, bf16[4,600,224]{1,2,0:T(8,128)(2,1)}, u32[]{:S(2)}) copy-start(bf16[4,600,224]{1,2,0:T(8,128)(2,1)} %copy-done.8) | copy-start | bytes 3225604
  99.2 8.8 %copy-start.10 = (f32[16,10]{1,0:T(8,128)S(1)}, f32[16,10]{1,0:T(8,128)}, u32[]{:S(2)}) copy-start(f32[16,10]{1,0:T(8,128)} %param.9) | copy-start | bytes 1924
  108.7 3.8 %copy-start.5 = (bf16[10,112,896]{2,1,0:T(8,128)(2,1)S(1)}, bf16[10,112,896]{2,1,0:T(8,128)(2,1)}, u32[]{:S(2)}) copy-start(bf16[10,112,896]{2,1,0:T(8,128)(2,1)} %copy-done.4) | copy-start | bytes 6021124
  108.7 26.6 %collective-permute-start.6 = (bf16[16,10]{1,0:T(8,128)(2,1)S(1)}, bf16[16,10]{1,0:T(8,128)(2,1)S(1)}, u32[]{:S(2)}, u32[]{:S(2)}) collective-permute-start(bf16[16,10]{1,0:T(8,128)(2,1)S(1)} %get-tuple-element.8), channel_id=1, source_target_pairs={{0,4},{12,8},{1,5},{13,9},{2,6},{14,10},{3,7},{15,11},{16,20},{28,... | collective-permute-start | bytes 968 | tf_op jit(solution)/shard_map/ppermute | solution.py:59
  112.5 1.6 copy-start.3
  137.7 22.7 %collective-permute-start.9 = (bf16[4,112,896]{2,0,1:T(4,128)(2,1)S(1)}, bf16[4,112,896]{2,0,1:T(4,128)(2,1)S(1)}, u32[]{:S(2)}, u32[]{:S(2)}) collective-permute-start(bf16[4,112,896]{2,0,1:T(4,128)(2,1)S(1)} %add_convert_fusion.5), channel_id=1, source_target_pairs={{4,8},{8,4},{5,9},{9,5},{6,10},{10,6},{7,11},{11,7},{20,24},{24,20... | collective-permute-start | bytes 2408456 | tf_op jit(solution)/shard_map/ppermute | solution.py:59
  142.9 57.5 %collective-permute-start.8 = (bf16[4,112,896]{2,0,1:T(4,128)(2,1)S(1)}, bf16[4,112,896]{2,0,1:T(4,128)(2,1)S(1)}, u32[]{:S(2)}, u32[]{:S(2)}) collective-permute-start(bf16[4,112,896]{2,0,1:T(4,128)(2,1)S(1)} %add_convert_fusion.7), channel_id=1, source_target_pairs={{4,8},{8,4},{5,9},{9,5},{6,10},{10,6},{7,11},{11,7},{20,24},{24,20... | collective-permute-start | bytes 2408456 | tf_op jit(solution)/shard_map/ppermute | solution.py:59
  148.8 46.0 %collective-permute-start.13 = (bf16[4,112,896]{2,0,1:T(4,128)(2,1)S(1)}, bf16[4,112,896]{2,0,1:T(4,128)(2,1)S(1)}, u32[]{:S(2)}, u32[]{:S(2)}) collective-permute-start(bf16[4,112,896]{2,0,1:T(4,128)(2,1)S(1)} %add_convert_fusion.1), channel_id=1, source_target_pairs={{4,8},{8,4},{5,9},{9,5},{6,10},{10,6},{7,11},{11,7},{20,24},{24,20... | collective-permute-start | bytes 2408456 | tf_op jit(solution)/shard_map/ppermute | solution.py:59
  162.9 37.6 %collective-permute-start.10 = (bf16[4,112,896]{2,0,1:T(4,128)(2,1)S(1)}, bf16[4,112,896]{2,0,1:T(4,128)(2,1)S(1)}, u32[]{:S(2)}, u32[]{:S(2)}) collective-permute-start(bf16[4,112,896]{2,0,1:T(4,128)(2,1)S(1)} %add_convert_fusion.4), channel_id=1, source_target_pairs={{4,0},{8,12},{5,1},{9,13},{6,2},{10,14},{7,3},{11,15},{20,16},{24,... | collective-permute-start | bytes 2408456 | tf_op jit(solution)/shard_map/ppermute | solution.py:59
  168.2 40.3 %collective-permute-start.12 = (bf16[4,112,896]{2,0,1:T(4,128)(2,1)}, bf16[4,112,896]{2,0,1:T(4,128)(2,1)}, u32[]{:S(2)}, u32[]{:S(2)}) collective-permute-start(bf16[4,112,896]{2,0,1:T(4,128)(2,1)} %add_convert_fusion.3), channel_id=1, source_target_pairs={{4,8},{8,4},{5,9},{9,5},{6,10},{10,6},{7,11},{11,7},{20,24},{24,20... | collective-permute-start | bytes 2408456 | tf_op jit(solution)/shard_map/ppermute | solution.py:59
  198.2 11.3 %collective-permute-start.14 = (bf16[4,112,896]{2,0,1:T(4,128)(2,1)}, bf16[4,112,896]{2,0,1:T(4,128)(2,1)}, u32[]{:S(2)}, u32[]{:S(2)}) collective-permute-start(bf16[4,112,896]{2,0,1:T(4,128)(2,1)} %add_convert_fusion), channel_id=1, source_target_pairs={{4,0},{8,12},{5,1},{9,13},{6,2},{10,14},{7,3},{11,15},{20,16},{24,... | collective-permute-start | bytes 2408456 | tf_op jit(solution)/shard_map/ppermute | solution.py:59
  204.1 15.3 %all-to-all-start.1 = ((bf16[4,112,896]{2,1,0:T(8,128)(2,1)}), bf16[4,112,896]{2,1,0:T(8,128)(2,1)S(1)}, u32[]{:S(2)}, u32[]{:S(2)}) async-start(bf16[4,112,896]{2,1,0:T(8,128)(2,1)} %copy.35), calls=%async_computation.1 | async-start | bytes 1605632 | tf_op jit(solution)/shard_map/all_to_all | solution.py:181
  219.4 5.8 %copy-start.7 = (bf16[4,112,896]{2,1,0:T(8,128)(2,1)}, bf16[4,112,896]{2,1,0:T(8,128)(2,1)S(1)}, u32[]{:S(2)}) copy-start(bf16[4,112,896]{2,1,0:T(8,128)(2,1)S(1)} %all-to-all-done.1) | copy-start | bytes 2408452
  219.4 16.1 %all-to-all-start.2 = ((bf16[4,112,896]{2,1,0:T(8,128)(2,1)}), bf16[4,112,896]{2,1,0:T(8,128)(2,1)}, u32[]{:S(2)}, u32[]{:S(2)}) async-start(bf16[4,112,896]{2,1,0:T(8,128)(2,1)} %copy.42), calls=%async_computation.2 | async-start | bytes 1605632 | tf_op jit(solution)/shard_map/all_to_all | solution.py:181
  245.1 1.0 copy-start.2
  246.1 22.5 %copy-start.1 = (bf16[10,600,224]{1,2,0:T(8,128)(2,1)S(1)}, bf16[10,600,224]{1,2,0:T(8,128)(2,1)}, u32[]{:S(2)}) copy-start(bf16[10,600,224]{1,2,0:T(8,128)(2,1)} %param.7) | copy-start | bytes 8064004
where the time goes:
time: 270 us; the launch traced here: 269 us
  waiting for transfers between devices  116 us (43%)
  starting transfers between devices  52.9 us (20%)
  matrix products  37.8 us (14%)
  blocking collectives  25.2 us (9%)
  local copies, waits for them, and re-layouts  21.9 us (8%)
  Pallas kernels  8.07 us (3%)
  other arithmetic  6.26 us (2%)
    ppermute x15, waiting for transfers between devices, go(): return lax.ppermute(array, 'chol', pairs)  99.3 us
    ppermute x15, starting transfers between devices, go(): return lax.ppermute(array, 'chol', pairs)  40.7 us
    dot_general x16, matrix products, rows_of(): jnp.einsum('wg,gpq->wpq', mine, chol_vec, preferred_element_type=jnp.floa...  28.4 us
    all_to_all x1, blocking collectives, body(): lax.all_to_all(blocks, 'orb', split_axis=0, concat_axis=0, tiled=True)  19 us
    all_to_all x2, waiting for transfers between devices, body(): lax.all_to_all(part, 'orb', split_axis=0, concat_axis=0, tiled=True)  16.3 us
    dot_general x4, matrix products, line_of_four(): jnp.einsum('wiq,giq->wg', block, half_chol, preferred_element_type=jnp.fl...  9.39 us
    pallas_call x1, Pallas kernels, taylor(): pl.pallas_call(taylor_kernel, out_shape=jax.ShapeDtypeStruct(held.shape,...  8.07 us
    all_to_all x2, starting transfers between devices, body(): lax.all_to_all(part, 'orb', split_axis=0, concat_axis=0, tiled=True)  7.91 us
  transfers between devices with their start and end apart: 18, of which 11 were waited for; matrix products, arithmetic and copies ran while one was open for 22% of the time, Pallas kernels for 0%

commit v1 on v0

--- a/solution.py
+++ b/solution.py
@@ -66,7 +66,7 @@
     l3 = go(l2, [(1, 0)])
     high = chol_vec.shape[1] // chunks
     own_chol, far_chol = [], []
-    after = (r1, l1)
+    after = (r2,)
     for c in range(chunks):
         part = chol_vec[:, c * high : (c + 1) * high]
         own_chol.append(part)

time: 270 us -> 268 us (level)
  matrix products: 37.8 us -> 32.9 us
    dot_general x16, matrix products: 28.4 us -> 23.4 us  [rows_of(): jnp.einsum('wg,gpq->wpq', mine, chol_vec, preferred_element_type=jnp.floa...]
  transfers between devices with their start and end apart: 18 -> 18, of which waited for: 11 -> 10; matrix products, arithmetic and copies ran while one was open for 22% -> 21% of each run, Pallas kernels for 0% -> 0%
where the time goes in v1:
time: 268 us; the launch traced here: 265 us
  waiting for transfers between devices  116 us (43%)
  starting transfers between devices  52.7 us (20%)
  matrix products  32.9 us (12%)
  blocking collectives  25.2 us (9%)
  local copies, waits for them, and re-layouts  21.5 us (8%)
  Pallas kernels  8.07 us (3%)
  other arithmetic  7.52 us (3%)
    ppermute x15, waiting for transfers between devices, go(): return lax.ppermute(array, 'chol', pairs)  102 us
    ppermute x15, starting transfers between devices, go(): return lax.ppermute(array, 'chol', pairs)  40.6 us
    dot_general x16, matrix products, rows_of(): jnp.einsum('wg,gpq->wpq', mine, chol_vec, preferred_element_type=jnp.floa...  23.4 us
    all_to_all x1, blocking collectives, body(): lax.all_to_all(blocks, 'orb', split_axis=0, concat_axis=0, tiled=True)  19 us
    all_to_all x2, waiting for transfers between devices, body(): lax.all_to_all(part, 'orb', split_axis=0, concat_axis=0, tiled=True)  14.5 us
    dot_general x4, matrix products, line_of_four(): jnp.einsum('wiq,giq->wg', block, half_chol, preferred_element_type=jnp.fl...  9.54 us
    optimization_barrier x4, local copies, waits for them, and re-layouts, line_of_four(): held_back = lax.optimization_barrier((part,) + after)[0]  8.31 us
    pallas_call x1, Pallas kernels, taylor(): pl.pallas_call(taylor_kernel, out_shape=jax.ShapeDtypeStruct(held.shape,...  8.07 us
  transfers between devices with their start and end apart: 18, of which 10 were waited for; matrix products, arithmetic and copies ran while one was open for 21% of the time, Pallas kernels for 0%

profile of v1, /device:TPU:8, one launch (start us, length us, event | category | flops | bytes accessed | tf_op | source)
XLA Modules:
  0.0 265.3 jit_solution(1144800039373430644)
XLA Ops:
  0.6 3.8 %collective-permute-start.1 = (bf16[4,600,224]{1,2,0:T(8,128)(2,1)}, bf16[4,600,224]{1,2,0:T(8,128)(2,1)}, u32[]{:S(2)}, u32[]{:S(2)}) collective-permute-start(bf16[4,600,224]{1,2,0:T(8,128)(2,1)} %param.6), channel_id=1, source_target_pairs={{0,4},{4,8},{8,12},{1,5},{5,9},{9,13},{2,6},{6,10},{10,14},{3,7},{... | collective-permute-start | bytes 3225608 | tf_op jit(solution)/shard_map/ppermute | solution.py:59
  4.4 3.4 %collective-permute-start = (bf16[4,600,224]{1,2,0:T(8,128)(2,1)}, bf16[4,600,224]{1,2,0:T(8,128)(2,1)}, u32[]{:S(2)}, u32[]{:S(2)}) collective-permute-start(bf16[4,600,224]{1,2,0:T(8,128)(2,1)} %param.6), channel_id=1, source_target_pairs={{4,0},{8,4},{12,8},{5,1},{9,5},{13,9},{6,2},{10,6},{14,10},{7,3},{... | collective-permute-start | bytes 3225608 | tf_op jit(solution)/shard_map/ppermute | solution.py:59
  7.8 22.3 %collective-permute-done.1 = bf16[4,600,224]{1,2,0:T(8,128)(2,1)} collective-permute-done((bf16[4,600,224]{1,2,0:T(8,128)(2,1)}, bf16[4,600,224]{1,2,0:T(8,128)(2,1)}, u32[]{:S(2)}, u32[]{:S(2)}) %collective-permute-start.1) | collective-permute-done | bytes 1075232 | tf_op jit(solution)/shard_map/ppermute | solution.py:59
  30.1 4.5 %collective-permute-start.2 = (bf16[4,600,224]{1,2,0:T(8,128)(2,1)}, bf16[4,600,224]{1,2,0:T(8,128)(2,1)}, u32[]{:S(2)}, u32[]{:S(2)}) collective-permute-start(bf16[4,600,224]{1,2,0:T(8,128)(2,1)} %collective-permute-done.1), channel_id=1, source_target_pairs={{4,8},{8,12},{5,9},{9,13},{6,10},{10,14},{7,11},{11,15},{20,24},{2... | collective-permute-start | bytes 3225608 | tf_op jit(solution)/shard_map/ppermute | solution.py:59
  34.6 2.1 collective-permute-start.4
  36.7 4.3 %all-to-all-start = ((bf16[4,600,224]{1,2,0:T(8,128)(2,1)}), bf16[4,600,224]{1,2,0:T(8,128)(2,1)}, u32[]{:S(2)}, u32[]{:S(2)}) async-start(bf16[4,600,224]{1,2,0:T(8,128)(2,1)} %param.11), calls=%async_computation | async-start | bytes 2293760 | tf_op jit(solution)/shard_map/all_to_all | solution.py:165
  41.0 16.6 %collective-permute-done.2 = bf16[4,600,224]{1,2,0:T(8,128)(2,1)} collective-permute-done((bf16[4,600,224]{1,2,0:T(8,128)(2,1)}, bf16[4,600,224]{1,2,0:T(8,128)(2,1)}, u32[]{:S(2)}, u32[]{:S(2)}) %collective-permute-start.2) | collective-permute-done | bytes 1075232 | tf_op jit(solution)/shard_map/ppermute | solution.py:59
  57.6 1.7 collective-permute-start.3
  59.2 4.5 %fusion.130 = (bf16[10,112,896]{2,1,0:T(8,128)(2,1)}, bf16[10,112,896]{2,1,0:T(8,128)(2,1)}) fusion(bf16[10,224,896]{2,1,0:T(8,128)(2,1)} %param.8), kind=kLoop, calls=%fused_computation.85 | loop fusion | bytes 8028160 | tf_op jit(solution)/shard_map/slice | solution.py:71
  63.7 4.0 %copy.45 = bf16[10,112,896]{2,0,1:T(8,128)(2,1)} copy(bf16[10,112,896]{2,1,0:T(8,128)(2,1)} %get-tuple-element.10) | data formatting | bytes 4014080 | tf_op jit(solution)/shard_map/optimization_barrier | solution.py:73
  67.7 2.2 copy.46
  71.4 3.4 %fusion.49 = f32[16,10]{1,0:T(8,128)S(1)} fusion(f32[16,10]{1,0:T(8,128)S(1)} %broadcast_in_dim.16, s32[]{:T(128)S(6)} %select_n.81, bf16[10,600,224]{1,2,0:T(8,128)(2,1)S(1)} %copy-done, bf16[4,600,224]{1,2,0:T(8,128)(2,1)} %param.6), kind=kOutput, calls=%fused_computation.39 | convolution fusion | flops 10752000 | bytes 3944452 | tf_op jit(solution)/shard_map/wiq,giq->wg/dot_general | solution.py:85
  74.8 1.7 copy.30
  77.8 1.9 add.110
  79.7 1.9 add.106
  81.6 2.0 fusion.59
  83.6 10.9 %collective-permute-done.5 = bf16[4,600,224]{1,2,0:T(8,128)(2,1)S(1)} collective-permute-done((bf16[4,600,224]{1,2,0:T(8,128)(2,1)}, bf16[4,600,224]{1,2,0:T(8,128)(2,1)S(1)}, u32[]{:S(2)}, u32[]{:S(2)}) %collective-permute-start.5) | collective-permute-done | bytes 1075232 | tf_op jit(solution)/shard_map/ppermute | solution.py:59
  94.5 1.5 add.114
  96.1 2.0 fusion.69
  98.1 2.0 fusion.79
  100.2 6.2 %psum.7 = f32[16,10]{1,0:T(8,128)S(1)} all-reduce(f32[16,10]{1,0:T(8,128)S(1)} %fusion.79), channel_id=1, replica_groups=mesh['grp'=2,'chol'=4,'orb'=4] {'orb'}, use_global_device_ids=true, to_apply=%region_0.1 | all-reduce | flops 160 | bytes 1280 | tf_op jit(solution)/shard_map/psum | solution.py:87
  109.0 2.2 fusion.96
  111.9 10.5 %collective-permute-done.7 = bf16[10,112,896]{2,1,0:T(8,128)(2,1)} collective-permute-done((bf16[10,112,896]{2,1,0:T(8,128)(2,1)}, bf16[10,112,896]{2,1,0:T(8,128)(2,1)}, u32[]{:S(2)}, u32[]{:S(2)}) %collective-permute-start.7) | collective-permute-done | bytes 2007072 | tf_op jit(solution)/shard_map/ppermute | solution.py:59
  122.8 1.5 collective-permute-start.11
  126.2 2.4 add_convert_fusion.5
  128.6 6.3 %collective-permute-start.9 = (bf16[4,112,896]{2,0,1:T(4,128)(2,1)S(1)}, bf16[4,112,896]{2,0,1:T(4,128)(2,1)S(1)}, u32[]{:S(2)}, u32[]{:S(2)}) collective-permute-start(bf16[4,112,896]{2,0,1:T(4,128)(2,1)S(1)} %add_convert_fusion.5), channel_id=1, source_target_pairs={{4,8},{8,4},{5,9},{9,5},{6,10},{10,6},{7,11},{11,7},{20,24},{24,20... | collective-permute-start | bytes 2408456 | tf_op jit(solution)/shard_map/ppermute | solution.py:59
  135.5 2.4 add_convert_fusion.7
  137.9 1.9 collective-permute-start.8
  139.9 27.5 %collective-permute-done.11 = bf16[10,112,896]{2,1,0:T(8,128)(2,1)S(1)} collective-permute-done((bf16[10,112,896]{2,1,0:T(8,128)(2,1)S(1)}, bf16[10,112,896]{2,1,0:T(8,128)(2,1)S(1)}, u32[]{:S(2)}, u32[]{:S(2)}) %collective-permute-start.11) | collective-permute-done | bytes 2007072 | tf_op jit(solution)/shard_map/ppermute | solution.py:59
  168.2 6.0 %collective-permute-start.13 = (bf16[4,112,896]{2,0,1:T(4,128)(2,1)S(1)}, bf16[4,112,896]{2,0,1:T(4,128)(2,1)S(1)}, u32[]{:S(2)}, u32[]{:S(2)}) collective-permute-start(bf16[4,112,896]{2,0,1:T(4,128)(2,1)S(1)} %add_convert_fusion.1), channel_id=1, source_target_pairs={{4,8},{8,4},{5,9},{9,5},{6,10},{10,6},{7,11},{11,7},{20,24},{24,20... | collective-permute-start | bytes 2408456 | tf_op jit(solution)/shard_map/ppermute | solution.py:59
  174.2 2.6 add_convert_fusion.4
  178.8 1.8 add_convert_fusion.3
  180.5 1.9 collective-permute-start.12
  182.5 10.6 %collective-permute-done.13 = bf16[4,112,896]{2,0,1:T(4,128)(2,1)S(1)} collective-permute-done((bf16[4,112,896]{2,0,1:T(4,128)(2,1)S(1)}, bf16[4,112,896]{2,0,1:T(4,128)(2,1)S(1)}, u32[]{:S(2)}, u32[]{:S(2)}) %collective-permute-start.13) | collective-permute-done | bytes 802848 | tf_op jit(solution)/shard_map/ppermute | solution.py:59
  193.0 1.9 add_convert_fusion
  194.9 2.2 collective-permute-start.14
  197.1 2.7 %fusion.100 = bf16[4,112,896]{2,0,1:T(4,128)(2,1)S(1)} fusion(bf16[4,112,896]{2,0,1:T(4,128)(2,1)S(1)} %collective-permute-done.10, f32[4,112,896]{2,0,1:T(4,128)S(1)} %fusion.96, bf16[10,112,896]{2,1,0:T(8,128)(2,1)} %collective-permute-done.7, bf16[4,112,896]{2,0,1:T(4,128)(2,1)S(1)} %collective-permute-done.8, pred[]{:T(512)S(6)} %and.26, ...), kind=kOutput, calls=%fused_computation.62 | convolution fusion | flops 10035200 | bytes 6022149 | tf_op jit(solution)/shard_map/wg,gpq->wpq/dot_general | solution.py:51
  200.8 3.7 %all-to-all-start.1 = ((bf16[4,112,896]{2,1,0:T(8,128)(2,1)}), bf16[4,112,896]{2,1,0:T(8,128)(2,1)S(1)}, u32[]{:S(2)}, u32[]{:S(2)}) async-start(bf16[4,112,896]{2,1,0:T(8,128)(2,1)} %copy.35), calls=%async_computation.1 | async-start | bytes 1605632 | tf_op jit(solution)/shard_map/all_to_all | solution.py:181
  205.5 3.1 %collective-permute-done.14 = bf16[4,112,896]{2,0,1:T(4,128)(2,1)} collective-permute-done((bf16[4,112,896]{2,0,1:T(4,128)(2,1)}, bf16[4,112,896]{2,0,1:T(4,128)(2,1)}, u32[]{:S(2)}, u32[]{:S(2)}) %collective-permute-start.14) | collective-permute-done | bytes 802848 | tf_op jit(solution)/shard_map/ppermute | solution.py:59
  208.6 2.3 fusion.103
  211.9 4.2 %all-to-all-done.1 = bf16[4,112,896]{2,1,0:T(8,128)(2,1)S(1)} async-done(((bf16[4,112,896]{2,1,0:T(8,128)(2,1)}), bf16[4,112,896]{2,1,0:T(8,128)(2,1)S(1)}, u32[]{:S(2)}, u32[]{:S(2)}) %all-to-all-start.1) | async-done | bytes 802848 | tf_op jit(solution)/shard_map/all_to_all | solution.py:181
  216.1 4.2 %all-to-all-start.2 = ((bf16[4,112,896]{2,1,0:T(8,128)(2,1)}), bf16[4,112,896]{2,1,0:T(8,128)(2,1)}, u32[]{:S(2)}, u32[]{:S(2)}) async-start(bf16[4,112,896]{2,1,0:T(8,128)(2,1)} %copy.42), calls=%async_computation.2 | async-start | bytes 1605632 | tf_op jit(solution)/shard_map/all_to_all | solution.py:181
  220.3 1.6 copy.43.held_ref
  221.9 10.3 %all-to-all-done.2 = bf16[4,112,896]{2,1,0:T(8,128)(2,1)} async-done(((bf16[4,112,896]{2,1,0:T(8,128)(2,1)}), bf16[4,112,896]{2,1,0:T(8,128)(2,1)}, u32[]{:S(2)}, u32[]{:S(2)}) %all-to-all-start.2) | async-done | bytes 802848 | tf_op jit(solution)/shard_map/all_to_all | solution.py:181
  232.2 1.5 pad_maximum_fusion
  233.7 8.1 %shard_map.77 = bf16[4,600,224]{2,1,0:T(8,128)(2,1)S(1)} custom-call(bf16[4,600,224]{2,1,0:T(8,128)(2,1)S(1)} %copy.43.held_ref, bf16[896,896]{1,0:T(8,128)(2,1)S(1)} %bitcast.49), custom_call_target="tpu_custom_call" | custom-call | flops 5780275200 | bytes 3225600 | tf_op jit(solution)/shard_map/pallas_call | solution.py:142
  242.8 2.5 copy.44
  245.3 19.0 %all_to_all.20 = bf16[4,600,224]{1,2,0:T(8,128)(2,1)S(1)} all-to-all(bf16[4,600,224]{1,2,0:T(8,128)(2,1)} %copy.44), channel_id=1, replica_groups=mesh['grp'=2,'chol'=4,'orb'=4] {'orb'}, dimensions={0} | all-to-all | bytes 2150400 | tf_op jit(solution)/shard_map/all_to_all | solution.py:186
  (57 shorter events, 16.7 us)
Async XLA Ops:
  0.6 70.7 %copy-start = (bf16[10,600,224]{1,2,0:T(8,128)(2,1)S(1)}, bf16[10,600,224]{1,2,0:T(8,128)(2,1)}, u32[]{:S(2)}) copy-start(bf16[10,600,224]{1,2,0:T(8,128)(2,1)} %param.7) | copy-start | bytes 8064004
  0.6 29.5 %collective-permute-start.1 = (bf16[4,600,224]{1,2,0:T(8,128)(2,1)}, bf16[4,600,224]{1,2,0:T(8,128)(2,1)}, u32[]{:S(2)}, u32[]{:S(2)}) collective-permute-start(bf16[4,600,224]{1,2,0:T(8,128)(2,1)} %param.6), channel_id=1, source_target_pairs={{0,4},{4,8},{8,12},{1,5},{5,9},{9,13},{2,6},{6,10},{10,14},{3,7},{... | collective-permute-start | bytes 3225608 | tf_op jit(solution)/shard_map/ppermute | solution.py:59
  4.4 30.2 %collective-permute-start = (bf16[4,600,224]{1,2,0:T(8,128)(2,1)}, bf16[4,600,224]{1,2,0:T(8,128)(2,1)}, u32[]{:S(2)}, u32[]{:S(2)}) collective-permute-start(bf16[4,600,224]{1,2,0:T(8,128)(2,1)} %param.6), channel_id=1, source_target_pairs={{4,0},{8,4},{12,8},{5,1},{9,5},{13,9},{6,2},{10,6},{14,10},{7,3},{... | collective-permute-start | bytes 3225608 | tf_op jit(solution)/shard_map/ppermute | solution.py:59
  30.1 27.4 %collective-permute-start.2 = (bf16[4,600,224]{1,2,0:T(8,128)(2,1)}, bf16[4,600,224]{1,2,0:T(8,128)(2,1)}, u32[]{:S(2)}, u32[]{:S(2)}) collective-permute-start(bf16[4,600,224]{1,2,0:T(8,128)(2,1)} %collective-permute-done.1), channel_id=1, source_target_pairs={{4,8},{8,12},{5,9},{9,13},{6,10},{10,14},{7,11},{11,15},{20,24},{2... | collective-permute-start | bytes 3225608 | tf_op jit(solution)/shard_map/ppermute | solution.py:59
  34.6 35.3 %collective-permute-start.4 = (bf16[4,600,224]{1,2,0:T(8,128)(2,1)}, bf16[4,600,224]{1,2,0:T(8,128)(2,1)}, u32[]{:S(2)}, u32[]{:S(2)}) collective-permute-start(bf16[4,600,224]{1,2,0:T(8,128)(2,1)} %collective-permute-done), channel_id=1, source_target_pairs={{8,4},{4,0},{9,5},{5,1},{10,6},{6,2},{11,7},{7,3},{24,20},{20,16},... | collective-permute-start | bytes 3225608 | tf_op jit(solution)/shard_map/ppermute | solution.py:59
  36.7 164.1 %all-to-all-start = ((bf16[4,600,224]{1,2,0:T(8,128)(2,1)}), bf16[4,600,224]{1,2,0:T(8,128)(2,1)}, u32[]{:S(2)}, u32[]{:S(2)}) async-start(bf16[4,600,224]{1,2,0:T(8,128)(2,1)} %param.11), calls=%async_computation | async-start | bytes 2293760 | tf_op jit(solution)/shard_map/all_to_all | solution.py:165
  57.6 22.1 %collective-permute-start.3 = (bf16[4,600,224]{1,2,0:T(8,128)(2,1)}, bf16[4,600,224]{1,2,0:T(8,128)(2,1)}, u32[]{:S(2)}, u32[]{:S(2)}) collective-permute-start(bf16[4,600,224]{1,2,0:T(8,128)(2,1)} %collective-permute-done.2), channel_id=1, source_target_pairs={{8,12},{9,13},{10,14},{11,15},{24,28},{25,29},{26,30},{27,31}} | collective-permute-start | bytes 3225608 | tf_op jit(solution)/shard_map/ppermute | solution.py:59
  63.7 4.0 %copy-start.3 = (bf16[10,112,896]{2,1,0:T(8,128)(2,1)S(1)}, bf16[10,112,896]{2,1,0:T(8,128)(2,1)}, u32[]{:S(2)}) copy-start(bf16[10,112,896]{2,1,0:T(8,128)(2,1)} %get-tuple-element.11) | copy-start | bytes 6021124
  67.7 2.2 copy-start.12
  69.9 24.6 %collective-permute-start.5 = (bf16[4,600,224]{1,2,0:T(8,128)(2,1)}, bf16[4,600,224]{1,2,0:T(8,128)(2,1)S(1)}, u32[]{:S(2)}, u32[]{:S(2)}) collective-permute-start(bf16[4,600,224]{1,2,0:T(8,128)(2,1)} %collective-permute-done.4), channel_id=1, source_target_pairs={{4,0},{5,1},{6,2},{7,3},{20,16},{21,17},{22,18},{23,19}} | collective-permute-start | bytes 3225608 | tf_op jit(solution)/shard_map/ppermute | solution.py:59
  71.3 3.4 %copy-start.9 = (bf16[10,112,896]{2,0,1:T(8,128)(2,1)S(1)}, bf16[10,112,896]{2,0,1:T(8,128)(2,1)}, u32[]{:S(2)}) copy-start(bf16[10,112,896]{2,0,1:T(8,128)(2,1)} %copy.45) | copy-start | bytes 6021124
  76.5 45.9 %collective-permute-start.7 = (bf16[10,112,896]{2,1,0:T(8,128)(2,1)}, bf16[10,112,896]{2,1,0:T(8,128)(2,1)}, u32[]{:S(2)}, u32[]{:S(2)}) collective-permute-start(bf16[10,112,896]{2,1,0:T(8,128)(2,1)} %copy.30), channel_id=1, source_target_pairs={{0,4},{12,8},{1,5},{13,9},{2,6},{14,10},{3,7},{15,11},{16,20},{28,... | collective-permute-start | bytes 6021128 | tf_op jit(solution)/shard_map/ppermute | solution.py:59
  98.1 8.8 %copy-start.11 = (f32[16,10]{1,0:T(8,128)S(1)}, f32[16,10]{1,0:T(8,128)}, u32[]{:S(2)}) copy-start(f32[16,10]{1,0:T(8,128)} %param.9) | copy-start | bytes 1924
  107.6 3.6 %copy-start.5 = (bf16[10,112,896]{2,1,0:T(8,128)(2,1)S(1)}, bf16[10,112,896]{2,1,0:T(8,128)(2,1)}, u32[]{:S(2)}) copy-start(bf16[10,112,896]{2,1,0:T(8,128)(2,1)} %get-tuple-element.10) | copy-start | bytes 6021124
  107.6 18.6 %collective-permute-start.6 = (bf16[16,10]{1,0:T(8,128)(2,1)S(1)}, bf16[16,10]{1,0:T(8,128)(2,1)S(1)}, u32[]{:S(2)}, u32[]{:S(2)}) collective-permute-start(bf16[16,10]{1,0:T(8,128)(2,1)S(1)} %get-tuple-element.8), channel_id=1, source_target_pairs={{0,4},{12,8},{1,5},{13,9},{2,6},{14,10},{3,7},{15,11},{16,20},{28,... | collective-permute-start | bytes 968 | tf_op jit(solution)/shard_map/ppermute | solution.py:59
  111.2 11.2 %copy-start.8 = (bf16[10,112,896]{2,0,1:T(8,128)(2,1)S(1)}, bf16[10,112,896]{2,0,1:T(8,128)(2,1)}, u32[]{:S(2)}) copy-start(bf16[10,112,896]{2,0,1:T(8,128)(2,1)} %copy.46) | copy-start | bytes 6021124
  111.9 12.4 %copy-start.4 = (bf16[10,112,896]{2,1,0:T(8,128)(2,1)S(1)}, bf16[10,112,896]{2,1,0:T(8,128)(2,1)}, u32[]{:S(2)}) copy-start(bf16[10,112,896]{2,1,0:T(8,128)(2,1)} %get-tuple-element.11) | copy-start | bytes 6021124
  122.8 44.6 %collective-permute-start.11 = (bf16[10,112,896]{2,1,0:T(8,128)(2,1)S(1)}, bf16[10,112,896]{2,1,0:T(8,128)(2,1)S(1)}, u32[]{:S(2)}, u32[]{:S(2)}) collective-permute-start(bf16[10,112,896]{2,1,0:T(8,128)(2,1)S(1)} %copy.37), channel_id=1, source_target_pairs={{0,4},{12,8},{1,5},{13,9},{2,6},{14,10},{3,7},{15,11},{16,20},{28,... | collective-permute-start | bytes 6021128 | tf_op jit(solution)/shard_map/ppermute | solution.py:59
  128.6 45.6 %collective-permute-start.9 = (bf16[4,112,896]{2,0,1:T(4,128)(2,1)S(1)}, bf16[4,112,896]{2,0,1:T(4,128)(2,1)S(1)}, u32[]{:S(2)}, u32[]{:S(2)}) collective-permute-start(bf16[4,112,896]{2,0,1:T(4,128)(2,1)S(1)} %add_convert_fusion.5), channel_id=1, source_target_pairs={{4,8},{8,4},{5,9},{9,5},{6,10},{10,6},{7,11},{11,7},{20,24},{24,20... | collective-permute-start | bytes 2408456 | tf_op jit(solution)/shard_map/ppermute | solution.py:59
  137.9 59.2 %collective-permute-start.8 = (bf16[4,112,896]{2,0,1:T(4,128)(2,1)S(1)}, bf16[4,112,896]{2,0,1:T(4,128)(2,1)S(1)}, u32[]{:S(2)}, u32[]{:S(2)}) collective-permute-start(bf16[4,112,896]{2,0,1:T(4,128)(2,1)S(1)} %add_convert_fusion.7), channel_id=1, source_target_pairs={{4,8},{8,4},{5,9},{9,5},{6,10},{10,6},{7,11},{11,7},{20,24},{24,20... | collective-permute-start | bytes 2408456 | tf_op jit(solution)/shard_map/ppermute | solution.py:59
  167.4 25.7 %copy-start.6 = (bf16[10,112,896]{2,1,0:T(8,128)(2,1)}, bf16[10,112,896]{2,1,0:T(8,128)(2,1)S(1)}, u32[]{:S(2)}) copy-start(bf16[10,112,896]{2,1,0:T(8,128)(2,1)S(1)} %collective-permute-done.11) | copy-start | bytes 6021124
  168.2 24.8 %collective-permute-start.13 = (bf16[4,112,896]{2,0,1:T(4,128)(2,1)S(1)}, bf16[4,112,896]{2,0,1:T(4,128)(2,1)S(1)}, u32[]{:S(2)}, u32[]{:S(2)}) collective-permute-start(bf16[4,112,896]{2,0,1:T(4,128)(2,1)S(1)} %add_convert_fusion.1), channel_id=1, source_target_pairs={{4,8},{8,4},{5,9},{9,5},{6,10},{10,6},{7,11},{11,7},{20,24},{24,20... | collective-permute-start | bytes 2408456 | tf_op jit(solution)/shard_map/ppermute | solution.py:59
  176.8 20.3 %collective-permute-start.10 = (bf16[4,112,896]{2,0,1:T(4,128)(2,1)S(1)}, bf16[4,112,896]{2,0,1:T(4,128)(2,1)S(1)}, u32[]{:S(2)}, u32[]{:S(2)}) collective-permute-start(bf16[4,112,896]{2,0,1:T(4,128)(2,1)S(1)} %add_convert_fusion.4), channel_id=1, source_target_pairs={{4,0},{8,12},{5,1},{9,13},{6,2},{10,14},{7,3},{11,15},{20,16},{24,... | collective-permute-start | bytes 2408456 | tf_op jit(solution)/shard_map/ppermute | solution.py:59
  180.5 24.9 %collective-permute-start.12 = (bf16[4,112,896]{2,0,1:T(4,128)(2,1)}, bf16[4,112,896]{2,0,1:T(4,128)(2,1)}, u32[]{:S(2)}, u32[]{:S(2)}) collective-permute-start(bf16[4,112,896]{2,0,1:T(4,128)(2,1)} %add_convert_fusion.3), channel_id=1, source_target_pairs={{4,8},{8,4},{5,9},{9,5},{6,10},{10,6},{7,11},{11,7},{20,24},{24,20... | collective-permute-start | bytes 2408456 | tf_op jit(solution)/shard_map/ppermute | solution.py:59
  194.9 13.6 %collective-permute-start.14 = (bf16[4,112,896]{2,0,1:T(4,128)(2,1)}, bf16[4,112,896]{2,0,1:T(4,128)(2,1)}, u32[]{:S(2)}, u32[]{:S(2)}) collective-permute-start(bf16[4,112,896]{2,0,1:T(4,128)(2,1)} %add_convert_fusion), channel_id=1, source_target_pairs={{4,0},{8,12},{5,1},{9,13},{6,2},{10,14},{7,3},{11,15},{20,16},{24,... | collective-permute-start | bytes 2408456 | tf_op jit(solution)/shard_map/ppermute | solution.py:59
  200.8 15.3 %all-to-all-start.1 = ((bf16[4,112,896]{2,1,0:T(8,128)(2,1)}), bf16[4,112,896]{2,1,0:T(8,128)(2,1)S(1)}, u32[]{:S(2)}, u32[]{:S(2)}) async-start(bf16[4,112,896]{2,1,0:T(8,128)(2,1)} %copy.35), calls=%async_computation.1 | async-start | bytes 1605632 | tf_op jit(solution)/shard_map/all_to_all | solution.py:181
  204.5 4.1 %copy-start.7 = (bf16[10,112,896]{2,1,0:T(8,128)(2,1)S(1)}, bf16[10,112,896]{2,1,0:T(8,128)(2,1)}, u32[]{:S(2)}) copy-start(bf16[10,112,896]{2,1,0:T(8,128)(2,1)} %copy-done.6) | copy-start | bytes 6021124
  216.1 5.8 %copy-start.10 = (bf16[4,112,896]{2,1,0:T(8,128)(2,1)}, bf16[4,112,896]{2,1,0:T(8,128)(2,1)S(1)}, u32[]{:S(2)}) copy-start(bf16[4,112,896]{2,1,0:T(8,128)(2,1)S(1)} %all-to-all-done.1) | copy-start | bytes 2408452
  216.1 16.1 %all-to-all-start.2 = ((bf16[4,112,896]{2,1,0:T(8,128)(2,1)}), bf16[4,112,896]{2,1,0:T(8,128)(2,1)}, u32[]{:S(2)}, u32[]{:S(2)}) async-start(bf16[4,112,896]{2,1,0:T(8,128)(2,1)} %copy.42), calls=%async_computation.2 | async-start | bytes 1605632 | tf_op jit(solution)/shard_map/all_to_all | solution.py:181
  241.8 1.0 copy-start.2
  242.8 22.5 %copy-start.1 = (bf16[10,600,224]{1,2,0:T(8,128)(2,1)S(1)}, bf16[10,600,224]{1,2,0:T(8,128)(2,1)}, u32[]{:S(2)}) copy-start(bf16[10,600,224]{1,2,0:T(8,128)(2,1)} %param.7) | copy-start | bytes 8064004

commit v2 on v1

--- a/solution.py
+++ b/solution.py
@@ -66,7 +66,7 @@
     l3 = go(l2, [(1, 0)])
     high = chol_vec.shape[1] // chunks
     own_chol, far_chol = [], []
-    after = (r2,)
+    after = (r1,)
     for c in range(chunks):
         part = chol_vec[:, c * high : (c + 1) * high]
         own_chol.append(part)

time: 268 us -> 270 us (level)
  matrix products: 32.9 us -> 37.8 us
    dot_general x16, matrix products: 23.4 us -> 28.4 us  [rows_of(): jnp.einsum('wg,gpq->wpq', mine, chol_vec, preferred_element_type=jnp.floa...]
  transfers between devices with their start and end apart: 18 -> 18, of which waited for: 10 -> 11; matrix products, arithmetic and copies ran while one was open for 21% -> 22% of each run, Pallas kernels for 0% -> 0%
where the time goes in v2:
time: 270 us; the launch traced here: 269 us
  waiting for transfers between devices  116 us (43%)
  starting transfers between devices  52.9 us (20%)
  matrix products  37.8 us (14%)
  blocking collectives  25.2 us (9%)
  local copies, waits for them, and re-layouts  21.9 us (8%)
  Pallas kernels  8.08 us (3%)
  other arithmetic  6.26 us (2%)
    ppermute x15, waiting for transfers between devices, go(): return lax.ppermute(array, 'chol', pairs)  99.3 us
    ppermute x15, starting transfers between devices, go(): return lax.ppermute(array, 'chol', pairs)  40.7 us
    dot_general x16, matrix products, rows_of(): jnp.einsum('wg,gpq->wpq', mine, chol_vec, preferred_element_type=jnp.floa...  28.4 us
    all_to_all x1, blocking collectives, body(): lax.all_to_all(blocks, 'orb', split_axis=0, concat_axis=0, tiled=True)  19 us
    all_to_all x2, waiting for transfers between devices, body(): lax.all_to_all(part, 'orb', split_axis=0, concat_axis=0, tiled=True)  16.3 us
    dot_general x4, matrix products, line_of_four(): jnp.einsum('wiq,giq->wg', block, half_chol, preferred_element_type=jnp.fl...  9.39 us
    pallas_call x1, Pallas kernels, taylor(): pl.pallas_call(taylor_kernel, out_shape=jax.ShapeDtypeStruct(held.shape,...  8.08 us
    all_to_all x2, starting transfers between devices, body(): lax.all_to_all(part, 'orb', split_axis=0, concat_axis=0, tiled=True)  7.91 us
  transfers between devices with their start and end apart: 18, of which 11 were waited for; matrix products, arithmetic and copies ran while one was open for 22% of the time, Pallas kernels for 0%

profile of v2, /device:TPU:8, one launch (start us, length us, event | category | flops | bytes accessed | tf_op | source)
XLA Modules:
  0.0 268.7 jit_solution(6943407525492268071)
XLA Ops:
  0.6 3.8 %collective-permute-start.1 = (bf16[4,600,224]{1,2,0:T(8,128)(2,1)}, bf16[4,600,224]{1,2,0:T(8,128)(2,1)S(1)}, u32[]{:S(2)}, u32[]{:S(2)}) collective-permute-start(bf16[4,600,224]{1,2,0:T(8,128)(2,1)} %param.6), channel_id=1, source_target_pairs={{0,4},{4,8},{8,12},{1,5},{5,9},{9,13},{2,6},{6,10},{10,14},{3,7},{... | collective-permute-start | bytes 3225608 | tf_op jit(solution)/shard_map/ppermute | solution.py:59
  4.4 2.4 collective-permute-start
  6.8 23.2 %collective-permute-done.1 = bf16[4,600,224]{1,2,0:T(8,128)(2,1)S(1)} collective-permute-done((bf16[4,600,224]{1,2,0:T(8,128)(2,1)}, bf16[4,600,224]{1,2,0:T(8,128)(2,1)S(1)}, u32[]{:S(2)}, u32[]{:S(2)}) %collective-permute-start.1) | collective-permute-done | bytes 1075232 | tf_op jit(solution)/shard_map/ppermute | solution.py:59
  30.0 4.5 %collective-permute-start.2 = (bf16[4,600,224]{1,2,0:T(8,128)(2,1)S(1)}, bf16[4,600,224]{1,2,0:T(8,128)(2,1)}, u32[]{:S(2)}, u32[]{:S(2)}) collective-permute-start(bf16[4,600,224]{1,2,0:T(8,128)(2,1)S(1)} %collective-permute-done.1), channel_id=1, source_target_pairs={{4,8},{8,12},{5,9},{9,13},{6,10},{10,14},{7,11},{11,15},{20,24},{2... | collective-permute-start | bytes 3225608 | tf_op jit(solution)/shard_map/ppermute | solution.py:59
  34.5 3.8 %fusion.130 = (bf16[10,112,896]{2,1,0:T(8,128)(2,1)S(1)}, bf16[10,112,896]{2,1,0:T(8,128)(2,1)}) fusion(bf16[10,224,896]{2,1,0:T(8,128)(2,1)} %param.8), kind=kLoop, calls=%fused_computation.85 | loop fusion | bytes 8028160 | tf_op jit(solution)/shard_map/slice | solution.py:71
  39.7 1.7 copy.30
  42.7 5.8 %collective-permute-start.4 = (bf16[4,600,224]{1,2,0:T(8,128)(2,1)}, bf16[4,600,224]{1,2,0:T(8,128)(2,1)}, u32[]{:S(2)}, u32[]{:S(2)}) collective-permute-start(bf16[4,600,224]{1,2,0:T(8,128)(2,1)} %collective-permute-done), channel_id=1, source_target_pairs={{8,4},{4,0},{9,5},{5,1},{10,6},{6,2},{11,7},{7,3},{24,20},{20,16},... | collective-permute-start | bytes 3225608 | tf_op jit(solution)/shard_map/ppermute | solution.py:59
  48.5 8.7 %collective-permute-done.2 = bf16[4,600,224]{1,2,0:T(8,128)(2,1)} collective-permute-done((bf16[4,600,224]{1,2,0:T(8,128)(2,1)S(1)}, bf16[4,600,224]{1,2,0:T(8,128)(2,1)}, u32[]{:S(2)}, u32[]{:S(2)}) %collective-permute-start.2) | collective-permute-done | bytes 1075232 | tf_op jit(solution)/shard_map/ppermute | solution.py:59
  57.2 1.7 collective-permute-start.3
  58.9 4.3 %all-to-all-start = ((bf16[4,600,224]{1,2,0:T(8,128)(2,1)}), bf16[4,600,224]{1,2,0:T(8,128)(2,1)}, u32[]{:S(2)}, u32[]{:S(2)}) async-start(bf16[4,600,224]{1,2,0:T(8,128)(2,1)} %param.11), calls=%async_computation | async-start | bytes 2293760 | tf_op jit(solution)/shard_map/all_to_all | solution.py:165
  63.2 3.8 %copy.46 = bf16[10,112,896]{2,0,1:T(8,128)(2,1)} copy(bf16[10,112,896]{2,1,0:T(8,128)(2,1)} %get-tuple-element.11) | data formatting | bytes 4014080 | tf_op jit(solution)/shard_map/optimization_barrier | solution.py:73
  67.1 3.3 %fusion.49 = f32[16,10]{1,0:T(8,128)S(1)} fusion(f32[16,10]{1,0:T(8,128)S(1)} %broadcast_in_dim.16, s32[]{:T(128)S(6)} %select_n.81, bf16[10,600,224]{1,2,0:T(8,128)(2,1)S(1)} %copy-done, bf16[4,600,224]{1,2,0:T(8,128)(2,1)} %param.6), kind=kOutput, calls=%fused_computation.39 | convolution fusion | flops 10752000 | bytes 3944452 | tf_op jit(solution)/shard_map/wiq,giq->wg/dot_general | solution.py:85
  70.4 1.6 collective-permute-done.4
  72.0 4.4 %collective-permute-start.5 = (bf16[4,600,224]{1,2,0:T(8,128)(2,1)}, bf16[4,600,224]{1,2,0:T(8,128)(2,1)S(1)}, u32[]{:S(2)}, u32[]{:S(2)}) collective-permute-start(bf16[4,600,224]{1,2,0:T(8,128)(2,1)} %collective-permute-done.4), channel_id=1, source_target_pairs={{4,0},{5,1},{6,2},{7,3},{20,16},{21,17},{22,18},{23,19}} | collective-permute-start | bytes 3225608 | tf_op jit(solution)/shard_map/ppermute | solution.py:59
  76.5 1.9 add.110
  78.4 9.6 %collective-permute-done.7 = bf16[10,112,896]{2,1,0:T(8,128)(2,1)} collective-permute-done((bf16[10,112,896]{2,1,0:T(8,128)(2,1)}, bf16[10,112,896]{2,1,0:T(8,128)(2,1)}, u32[]{:S(2)}, u32[]{:S(2)}) %collective-permute-start.7) | collective-permute-done | bytes 2007072 | tf_op jit(solution)/shard_map/ppermute | solution.py:59
  88.0 1.7 copy.37
  90.9 1.9 add.106
  92.8 2.0 fusion.59
  94.8 2.0 fusion.69
  96.9 2.1 collective-permute-done.5
  99.3 2.0 fusion.79
  101.3 6.2 %psum.7 = f32[16,10]{1,0:T(8,128)S(1)} all-reduce(f32[16,10]{1,0:T(8,128)S(1)} %fusion.79), channel_id=1, replica_groups=mesh['grp'=2,'chol'=4,'orb'=4] {'orb'}, use_global_device_ids=true, to_apply=%region_0.1 | all-reduce | flops 160 | bytes 1280 | tf_op jit(solution)/shard_map/psum | solution.py:87
  108.7 1.6 collective-permute-start.6
  110.3 2.2 fusion.96
  116.0 19.3 %collective-permute-done.6 = bf16[16,10]{1,0:T(8,128)(2,1)S(1)} collective-permute-done((bf16[16,10]{1,0:T(8,128)(2,1)S(1)}, bf16[16,10]{1,0:T(8,128)(2,1)S(1)}, u32[]{:S(2)}, u32[]{:S(2)}) %collective-permute-start.6) | collective-permute-done | bytes 352 | tf_op jit(solution)/shard_map/ppermute | solution.py:59
  135.3 2.3 add_convert_fusion.5
  137.7 2.3 collective-permute-start.9
  140.6 2.3 add_convert_fusion.7
  142.9 3.6 %collective-permute-start.8 = (bf16[4,112,896]{2,0,1:T(4,128)(2,1)S(1)}, bf16[4,112,896]{2,0,1:T(4,128)(2,1)S(1)}, u32[]{:S(2)}, u32[]{:S(2)}) collective-permute-start(bf16[4,112,896]{2,0,1:T(4,128)(2,1)S(1)} %add_convert_fusion.7), channel_id=1, source_target_pairs={{4,8},{8,4},{5,9},{9,5},{6,10},{10,6},{7,11},{11,7},{20,24},{24,20... | collective-permute-start | bytes 2408456 | tf_op jit(solution)/shard_map/ppermute | solution.py:59
  146.5 2.3 add_convert_fusion.1
  148.8 2.3 collective-permute-start.13
  151.1 9.3 %collective-permute-done.9 = bf16[4,112,896]{2,0,1:T(4,128)(2,1)S(1)} collective-permute-done((bf16[4,112,896]{2,0,1:T(4,128)(2,1)S(1)}, bf16[4,112,896]{2,0,1:T(4,128)(2,1)S(1)}, u32[]{:S(2)}, u32[]{:S(2)}) %collective-permute-start.9) | collective-permute-done | bytes 802848 | tf_op jit(solution)/shard_map/ppermute | solution.py:59
  160.4 2.5 add_convert_fusion.4
  164.9 3.3 %add_convert_fusion.3 = bf16[4,112,896]{2,0,1:T(4,128)(2,1)} fusion(f32[4,112,896]{2,0,1:T(4,128)S(1)} %fusion.90, bf16[10,112,896]{2,1,0:T(8,128)(2,1)} %collective-permute-done.11, bf16[16,10]{1,0:T(8,128)(2,1)S(1)} %collective-permute-done.6, s32[]{:T(128)S(6)} %select_n.91), kind=kOutput, calls=%fused_computation.29 | convolution fusion | flops 8830976 | bytes 4416516 | tf_op jit(solution)/shard_map/wg,gpq->wpq/dot_general | solution.py:51
  168.1 2.3 collective-permute-start.12
  170.4 24.4 %collective-permute-done.13 = bf16[4,112,896]{2,0,1:T(4,128)(2,1)S(1)} collective-permute-done((bf16[4,112,896]{2,0,1:T(4,128)(2,1)S(1)}, bf16[4,112,896]{2,0,1:T(4,128)(2,1)S(1)}, u32[]{:S(2)}, u32[]{:S(2)}) %collective-permute-start.13) | collective-permute-done | bytes 802848 | tf_op jit(solution)/shard_map/ppermute | solution.py:59
  194.8 3.4 %add_convert_fusion = bf16[4,112,896]{2,0,1:T(4,128)(2,1)} fusion(f32[4,112,896]{2,0,1:T(4,128)S(1)} %fusion.84, bf16[4,112,896]{2,0,1:T(4,128)(2,1)S(1)} %collective-permute-done.13, bf16[10,112,896]{2,1,0:T(8,128)(2,1)} %collective-permute-done.11, bf16[16,10]{1,0:T(8,128)(2,1)S(1)} %collective-permute-done.6, s32[]{:T(128)S(6)} %select_n.95), kind=kOutput, calls=%fused_computation.26 | convolution fusion | flops 9633792 | bytes 5219332 | tf_op jit(solution)/shard_map/wg,gpq->wpq/dot_general | solution.py:51
  198.2 2.2 collective-permute-start.14
  200.4 2.7 fusion.100
  204.1 3.7 %all-to-all-start.1 = ((bf16[4,112,896]{2,1,0:T(8,128)(2,1)}), bf16[4,112,896]{2,1,0:T(8,128)(2,1)S(1)}, u32[]{:S(2)}, u32[]{:S(2)}) async-start(bf16[4,112,896]{2,1,0:T(8,128)(2,1)} %copy.35), calls=%async_computation.1 | async-start | bytes 1605632 | tf_op jit(solution)/shard_map/all_to_all | solution.py:181
  209.5 2.9 %fusion.103 = bf16[4,112,896]{2,0,1:T(4,128)(2,1)S(1)} fusion(bf16[4,112,896]{2,0,1:T(4,128)(2,1)} %collective-permute-done.14, f32[4,112,896]{2,0,1:T(4,128)S(1)} %fusion.88, bf16[10,112,896]{2,1,0:T(8,128)(2,1)} %collective-permute-done.11, bf16[4,112,896]{2,0,1:T(4,128)(2,1)} %collective-permute-done.12, pred[]{:T(512)S(6)} %and.26, ...), kind=kOutput, calls=%fused_computation.63 | convolution fusion | flops 10035200 | bytes 6022149 | tf_op jit(solution)/shard_map/wg,gpq->wpq/dot_general | solution.py:51
  213.4 6.0 %all-to-all-done.1 = bf16[4,112,896]{2,1,0:T(8,128)(2,1)S(1)} async-done(((bf16[4,112,896]{2,1,0:T(8,128)(2,1)}), bf16[4,112,896]{2,1,0:T(8,128)(2,1)S(1)}, u32[]{:S(2)}, u32[]{:S(2)}) %all-to-all-start.1) | async-done | bytes 802848 | tf_op jit(solution)/shard_map/all_to_all | solution.py:181
  219.4 4.2 %all-to-all-start.2 = ((bf16[4,112,896]{2,1,0:T(8,128)(2,1)}), bf16[4,112,896]{2,1,0:T(8,128)(2,1)}, u32[]{:S(2)}, u32[]{:S(2)}) async-start(bf16[4,112,896]{2,1,0:T(8,128)(2,1)} %copy.42), calls=%async_computation.2 | async-start | bytes 1605632 | tf_op jit(solution)/shard_map/all_to_all | solution.py:181
  225.2 10.3 %all-to-all-done.2 = bf16[4,112,896]{2,1,0:T(8,128)(2,1)} async-done(((bf16[4,112,896]{2,1,0:T(8,128)(2,1)}), bf16[4,112,896]{2,1,0:T(8,128)(2,1)}, u32[]{:S(2)}, u32[]{:S(2)}) %all-to-all-start.2) | async-done | bytes 802848 | tf_op jit(solution)/shard_map/all_to_all | solution.py:181
  237.0 8.1 %shard_map.77 = bf16[4,600,224]{2,1,0:T(8,128)(2,1)S(1)} custom-call(bf16[4,600,224]{2,1,0:T(8,128)(2,1)S(1)} %copy.43.held_ref, bf16[896,896]{1,0:T(8,128)(2,1)S(1)} %bitcast.49), custom_call_target="tpu_custom_call" | custom-call | flops 5780275200 | bytes 3225600 | tf_op jit(solution)/shard_map/pallas_call | solution.py:142
  246.1 2.5 copy.44
  248.6 19.0 %all_to_all.20 = bf16[4,600,224]{1,2,0:T(8,128)(2,1)S(1)} all-to-all(bf16[4,600,224]{1,2,0:T(8,128)(2,1)} %copy.44), channel_id=1, replica_groups=mesh['grp'=2,'chol'=4,'orb'=4] {'orb'}, dimensions={0} | all-to-all | bytes 2150400 | tf_op jit(solution)/shard_map/all_to_all | solution.py:186
  (55 shorter events, 20.4 us)
Async XLA Ops:
  0.6 66.4 %copy-start = (bf16[10,600,224]{1,2,0:T(8,128)(2,1)S(1)}, bf16[10,600,224]{1,2,0:T(8,128)(2,1)}, u32[]{:S(2)}) copy-start(bf16[10,600,224]{1,2,0:T(8,128)(2,1)} %param.7) | copy-start | bytes 8064004
  0.6 29.4 %collective-permute-start.1 = (bf16[4,600,224]{1,2,0:T(8,128)(2,1)}, bf16[4,600,224]{1,2,0:T(8,128)(2,1)S(1)}, u32[]{:S(2)}, u32[]{:S(2)}) collective-permute-start(bf16[4,600,224]{1,2,0:T(8,128)(2,1)} %param.6), channel_id=1, source_target_pairs={{0,4},{4,8},{8,12},{1,5},{5,9},{9,13},{2,6},{6,10},{10,14},{3,7},{... | collective-permute-start | bytes 3225608 | tf_op jit(solution)/shard_map/ppermute | solution.py:59
  4.4 38.2 %collective-permute-start = (bf16[4,600,224]{1,2,0:T(8,128)(2,1)}, bf16[4,600,224]{1,2,0:T(8,128)(2,1)}, u32[]{:S(2)}, u32[]{:S(2)}) collective-permute-start(bf16[4,600,224]{1,2,0:T(8,128)(2,1)} %param.6), channel_id=1, source_target_pairs={{4,0},{8,4},{12,8},{5,1},{9,5},{13,9},{6,2},{10,6},{14,10},{7,3},{... | collective-permute-start | bytes 3225608 | tf_op jit(solution)/shard_map/ppermute | solution.py:59
  30.0 8.3 %copy-start.8 = (bf16[4,600,224]{1,2,0:T(8,128)(2,1)}, bf16[4,600,224]{1,2,0:T(8,128)(2,1)S(1)}, u32[]{:S(2)}) copy-start(bf16[4,600,224]{1,2,0:T(8,128)(2,1)S(1)} %collective-permute-done.1) | copy-start | bytes 3225604
  30.0 27.2 %collective-permute-start.2 = (bf16[4,600,224]{1,2,0:T(8,128)(2,1)S(1)}, bf16[4,600,224]{1,2,0:T(8,128)(2,1)}, u32[]{:S(2)}, u32[]{:S(2)}) collective-permute-start(bf16[4,600,224]{1,2,0:T(8,128)(2,1)S(1)} %collective-permute-done.1), channel_id=1, source_target_pairs={{4,8},{8,12},{5,9},{9,13},{6,10},{10,14},{7,11},{11,15},{20,24},{2... | collective-permute-start | bytes 3225608 | tf_op jit(solution)/shard_map/ppermute | solution.py:59
  38.3 1.4 copy-start.4
  41.4 46.6 %collective-permute-start.7 = (bf16[10,112,896]{2,1,0:T(8,128)(2,1)}, bf16[10,112,896]{2,1,0:T(8,128)(2,1)}, u32[]{:S(2)}, u32[]{:S(2)}) collective-permute-start(bf16[10,112,896]{2,1,0:T(8,128)(2,1)} %copy.30), channel_id=1, source_target_pairs={{0,4},{12,8},{1,5},{13,9},{2,6},{14,10},{3,7},{15,11},{16,20},{28,... | collective-permute-start | bytes 6021128 | tf_op jit(solution)/shard_map/ppermute | solution.py:59
  42.7 29.3 %collective-permute-start.4 = (bf16[4,600,224]{1,2,0:T(8,128)(2,1)}, bf16[4,600,224]{1,2,0:T(8,128)(2,1)}, u32[]{:S(2)}, u32[]{:S(2)}) collective-permute-start(bf16[4,600,224]{1,2,0:T(8,128)(2,1)} %collective-permute-done), channel_id=1, source_target_pairs={{8,4},{4,0},{9,5},{5,1},{10,6},{6,2},{11,7},{7,3},{24,20},{20,16},... | collective-permute-start | bytes 3225608 | tf_op jit(solution)/shard_map/ppermute | solution.py:59
  57.2 33.7 %collective-permute-start.3 = (bf16[4,600,224]{1,2,0:T(8,128)(2,1)}, bf16[4,600,224]{1,2,0:T(8,128)(2,1)}, u32[]{:S(2)}, u32[]{:S(2)}) collective-permute-start(bf16[4,600,224]{1,2,0:T(8,128)(2,1)} %collective-permute-done.2), channel_id=1, source_target_pairs={{8,12},{9,13},{10,14},{11,15},{24,28},{25,29},{26,30},{27,31}} | collective-permute-start | bytes 3225608 | tf_op jit(solution)/shard_map/ppermute | solution.py:59
  58.9 145.2 %all-to-all-start = ((bf16[4,600,224]{1,2,0:T(8,128)(2,1)}), bf16[4,600,224]{1,2,0:T(8,128)(2,1)}, u32[]{:S(2)}, u32[]{:S(2)}) async-start(bf16[4,600,224]{1,2,0:T(8,128)(2,1)} %param.11), calls=%async_computation | async-start | bytes 2293760 | tf_op jit(solution)/shard_map/all_to_all | solution.py:165
  63.2 3.8 %copy-start.11 = (s32[16]{0:T(128)S(1)}, s32[16]{0:T(128)}, u32[]{:S(2)}) copy-start(s32[16]{0:T(128)} %param.10) | copy-start | bytes 196
  70.4 17.6 %copy-start.6 = (bf16[10,112,896]{2,0,1:T(8,128)(2,1)S(1)}, bf16[10,112,896]{2,0,1:T(8,128)(2,1)}, u32[]{:S(2)}) copy-start(bf16[10,112,896]{2,0,1:T(8,128)(2,1)} %copy.46) | copy-start | bytes 6021124
  72.0 27.0 %collective-permute-start.5 = (bf16[4,600,224]{1,2,0:T(8,128)(2,1)}, bf16[4,600,224]{1,2,0:T(8,128)(2,1)S(1)}, u32[]{:S(2)}, u32[]{:S(2)}) collective-permute-start(bf16[4,600,224]{1,2,0:T(8,128)(2,1)} %collective-permute-done.4), channel_id=1, source_target_pairs={{4,0},{5,1},{6,2},{7,3},{20,16},{21,17},{22,18},{23,19}} | collective-permute-start | bytes 3225608 | tf_op jit(solution)/shard_map/ppermute | solution.py:59
  89.6 56.9 %collective-permute-start.11 = (bf16[10,112,896]{2,1,0:T(8,128)(2,1)}, bf16[10,112,896]{2,1,0:T(8,128)(2,1)}, u32[]{:S(2)}, u32[]{:S(2)}) collective-permute-start(bf16[10,112,896]{2,1,0:T(8,128)(2,1)} %copy.37), channel_id=1, source_target_pairs={{0,4},{12,8},{1,5},{13,9},{2,6},{14,10},{3,7},{15,11},{16,20},{28,... | collective-permute-start | bytes 6021128 | tf_op jit(solution)/shard_map/ppermute | solution.py:59
  94.8 4.1 %copy-start.9 = (bf16[4,600,224]{1,2,0:T(8,128)(2,1)S(1)}, bf16[4,600,224]{1,2,0:T(8,128)(2,1)}, u32[]{:S(2)}) copy-start(bf16[4,600,224]{1,2,0:T(8,128)(2,1)} %copy-done.8) | copy-start | bytes 3225604
  99.2 8.8 %copy-start.10 = (f32[16,10]{1,0:T(8,128)S(1)}, f32[16,10]{1,0:T(8,128)}, u32[]{:S(2)}) copy-start(f32[16,10]{1,0:T(8,128)} %param.9) | copy-start | bytes 1924
  108.7 3.8 %copy-start.5 = (bf16[10,112,896]{2,1,0:T(8,128)(2,1)S(1)}, bf16[10,112,896]{2,1,0:T(8,128)(2,1)}, u32[]{:S(2)}) copy-start(bf16[10,112,896]{2,1,0:T(8,128)(2,1)} %copy-done.4) | copy-start | bytes 6021124
  108.7 26.6 %collective-permute-start.6 = (bf16[16,10]{1,0:T(8,128)(2,1)S(1)}, bf16[16,10]{1,0:T(8,128)(2,1)S(1)}, u32[]{:S(2)}, u32[]{:S(2)}) collective-permute-start(bf16[16,10]{1,0:T(8,128)(2,1)S(1)} %get-tuple-element.8), channel_id=1, source_target_pairs={{0,4},{12,8},{1,5},{13,9},{2,6},{14,10},{3,7},{15,11},{16,20},{28,... | collective-permute-start | bytes 968 | tf_op jit(solution)/shard_map/ppermute | solution.py:59
  112.5 1.6 copy-start.3
  137.7 22.7 %collective-permute-start.9 = (bf16[4,112,896]{2,0,1:T(4,128)(2,1)S(1)}, bf16[4,112,896]{2,0,1:T(4,128)(2,1)S(1)}, u32[]{:S(2)}, u32[]{:S(2)}) collective-permute-start(bf16[4,112,896]{2,0,1:T(4,128)(2,1)S(1)} %add_convert_fusion.5), channel_id=1, source_target_pairs={{4,8},{8,4},{5,9},{9,5},{6,10},{10,6},{7,11},{11,7},{20,24},{24,20... | collective-permute-start | bytes 2408456 | tf_op jit(solution)/shard_map/ppermute | solution.py:59
  142.9 57.5 %collective-permute-start.8 = (bf16[4,112,896]{2,0,1:T(4,128)(2,1)S(1)}, bf16[4,112,896]{2,0,1:T(4,128)(2,1)S(1)}, u32[]{:S(2)}, u32[]{:S(2)}) collective-permute-start(bf16[4,112,896]{2,0,1:T(4,128)(2,1)S(1)} %add_convert_fusion.7), channel_id=1, source_target_pairs={{4,8},{8,4},{5,9},{9,5},{6,10},{10,6},{7,11},{11,7},{20,24},{24,20... | collective-permute-start | bytes 2408456 | tf_op jit(solution)/shard_map/ppermute | solution.py:59
  148.8 46.0 %collective-permute-start.13 = (bf16[4,112,896]{2,0,1:T(4,128)(2,1)S(1)}, bf16[4,112,896]{2,0,1:T(4,128)(2,1)S(1)}, u32[]{:S(2)}, u32[]{:S(2)}) collective-permute-start(bf16[4,112,896]{2,0,1:T(4,128)(2,1)S(1)} %add_convert_fusion.1), channel_id=1, source_target_pairs={{4,8},{8,4},{5,9},{9,5},{6,10},{10,6},{7,11},{11,7},{20,24},{24,20... | collective-permute-start | bytes 2408456 | tf_op jit(solution)/shard_map/ppermute | solution.py:59
  162.9 37.6 %collective-permute-start.10 = (bf16[4,112,896]{2,0,1:T(4,128)(2,1)S(1)}, bf16[4,112,896]{2,0,1:T(4,128)(2,1)S(1)}, u32[]{:S(2)}, u32[]{:S(2)}) collective-permute-start(bf16[4,112,896]{2,0,1:T(4,128)(2,1)S(1)} %add_convert_fusion.4), channel_id=1, source_target_pairs={{4,0},{8,12},{5,1},{9,13},{6,2},{10,14},{7,3},{11,15},{20,16},{24,... | collective-permute-start | bytes 2408456 | tf_op jit(solution)/shard_map/ppermute | solution.py:59
  168.1 40.3 %collective-permute-start.12 = (bf16[4,112,896]{2,0,1:T(4,128)(2,1)}, bf16[4,112,896]{2,0,1:T(4,128)(2,1)}, u32[]{:S(2)}, u32[]{:S(2)}) collective-permute-start(bf16[4,112,896]{2,0,1:T(4,128)(2,1)} %add_convert_fusion.3), channel_id=1, source_target_pairs={{4,8},{8,4},{5,9},{9,5},{6,10},{10,6},{7,11},{11,7},{20,24},{24,20... | collective-permute-start | bytes 2408456 | tf_op jit(solution)/shard_map/ppermute | solution.py:59
  198.2 11.3 %collective-permute-start.14 = (bf16[4,112,896]{2,0,1:T(4,128)(2,1)}, bf16[4,112,896]{2,0,1:T(4,128)(2,1)}, u32[]{:S(2)}, u32[]{:S(2)}) collective-permute-start(bf16[4,112,896]{2,0,1:T(4,128)(2,1)} %add_convert_fusion), channel_id=1, source_target_pairs={{4,0},{8,12},{5,1},{9,13},{6,2},{10,14},{7,3},{11,15},{20,16},{24,... | collective-permute-start | bytes 2408456 | tf_op jit(solution)/shard_map/ppermute | solution.py:59
  204.1 15.3 %all-to-all-start.1 = ((bf16[4,112,896]{2,1,0:T(8,128)(2,1)}), bf16[4,112,896]{2,1,0:T(8,128)(2,1)S(1)}, u32[]{:S(2)}, u32[]{:S(2)}) async-start(bf16[4,112,896]{2,1,0:T(8,128)(2,1)} %copy.35), calls=%async_computation.1 | async-start | bytes 1605632 | tf_op jit(solution)/shard_map/all_to_all | solution.py:181
  219.4 5.8 %copy-start.7 = (bf16[4,112,896]{2,1,0:T(8,128)(2,1)}, bf16[4,112,896]{2,1,0:T(8,128)(2,1)S(1)}, u32[]{:S(2)}) copy-start(bf16[4,112,896]{2,1,0:T(8,128)(2,1)S(1)} %all-to-all-done.1) | copy-start | bytes 2408452
  219.4 16.1 %all-to-all-start.2 = ((bf16[4,112,896]{2,1,0:T(8,128)(2,1)}), bf16[4,112,896]{2,1,0:T(8,128)(2,1)}, u32[]{:S(2)}, u32[]{:S(2)}) async-start(bf16[4,112,896]{2,1,0:T(8,128)(2,1)} %copy.42), calls=%async_computation.2 | async-start | bytes 1605632 | tf_op jit(solution)/shard_map/all_to_all | solution.py:181
  245.1 1.0 copy-start.2
  246.1 22.5 %copy-start.1 = (bf16[10,600,224]{1,2,0:T(8,128)(2,1)S(1)}, bf16[10,600,224]{1,2,0:T(8,128)(2,1)}, u32[]{:S(2)}) copy-start(bf16[10,600,224]{1,2,0:T(8,128)(2,1)} %param.7) | copy-start | bytes 8064004

commit v3 on v2

--- a/solution.py
+++ b/solution.py
@@ -64,11 +64,12 @@
     l2 = go(l1, [(2, 1), (1, 0)])
     r3 = go(r2, [(2, 3)])
     l3 = go(l2, [(1, 0)])
-    high = chol_vec.shape[1] // chunks
+    tall = chol_vec.shape[1]
+    edges = [0, tall] if chunks == 1 else [0, -(-tall * 5 // 8 // 16) * 16, tall]
     own_chol, far_chol = [], []
     after = (r1,)
     for c in range(chunks):
-        part = chol_vec[:, c * high : (c + 1) * high]
+        part = chol_vec[:, edges[c] : edges[c + 1]]
         own_chol.append(part)
         held_back = lax.optimization_barrier((part,) + after)[0]
         got = go(held_back, [(0, 1), (3, 2)])

time: 270 us -> 282 us (1.044)
  waiting for transfers between devices: 116 us -> 134 us
  matrix products: 37.8 us -> 31.4 us
  starting transfers between devices: 52.9 us -> 49.7 us
    ppermute x15, waiting for transfers between devices: 99.3 us -> 116 us  [go(): return lax.ppermute(array, 'chol', pairs)]
    dot_general x16, matrix products: 28.4 us -> 21.9 us  [rows_of(): jnp.einsum('wg,gpq->wpq', mine, chol_vec, preferred_element_type=jnp.floa...]
    ppermute x15, starting transfers between devices: 40.7 us -> 37.7 us  [go(): return lax.ppermute(array, 'chol', pairs)]
  transfers between devices with their start and end apart: 18 -> 18, of which waited for: 11 -> 9; matrix products, arithmetic and copies ran while one was open for 22% -> 19% of each run, Pallas kernels for 0% -> 0%
where the time goes in v3:
time: 282 us; the launch traced here: 281 us
  waiting for transfers between devices  134 us (48%)
  starting transfers between devices  49.7 us (18%)
  matrix products  31.4 us (11%)
  blocking collectives  26.1 us (9%)
  local copies, waits for them, and re-layouts  22.3 us (8%)
  Pallas kernels  8.07 us (3%)
  other arithmetic  7.57 us (3%)
    ppermute x15, waiting for transfers between devices, go(): return lax.ppermute(array, 'chol', pairs)  116 us
    ppermute x15, starting transfers between devices, go(): return lax.ppermute(array, 'chol', pairs)  37.7 us
    dot_general x16, matrix products, rows_of(): jnp.einsum('wg,gpq->wpq', mine, chol_vec, preferred_element_type=jnp.floa...  21.9 us
    all_to_all x1, blocking collectives, body(): lax.all_to_all(blocks, 'orb', split_axis=0, concat_axis=0, tiled=True)  19 us
    all_to_all x2, waiting for transfers between devices, body(): lax.all_to_all(part, 'orb', split_axis=0, concat_axis=0, tiled=True)  17.8 us
    dot_general x4, matrix products, line_of_four(): jnp.einsum('wiq,giq->wg', block, half_chol, preferred_element_type=jnp.fl...  9.54 us
    pallas_call x1, Pallas kernels, taylor(): pl.pallas_call(taylor_kernel, out_shape=jax.ShapeDtypeStruct(held.shape,...  8.07 us
    all_to_all x2, starting transfers between devices, body(): lax.all_to_all(part, 'orb', split_axis=0, concat_axis=0, tiled=True)  7.71 us
  transfers between devices with their start and end apart: 18, of which 9 were waited for; matrix products, arithmetic and copies ran while one was open for 19% of the time, Pallas kernels for 0%

profile of v3, /device:TPU:8, one launch (start us, length us, event | category | flops | bytes accessed | tf_op | source)
XLA Modules:
  0.0 280.5 jit_solution(9758821422299179425)
XLA Ops:
  0.6 3.8 %collective-permute-start.1 = (bf16[4,600,224]{1,2,0:T(8,128)(2,1)}, bf16[4,600,224]{1,2,0:T(8,128)(2,1)S(1)}, u32[]{:S(2)}, u32[]{:S(2)}) collective-permute-start(bf16[4,600,224]{1,2,0:T(8,128)(2,1)} %param.6), channel_id=1, source_target_pairs={{0,4},{4,8},{8,12},{1,5},{5,9},{9,13},{2,6},{6,10},{10,14},{3,7},{... | collective-permute-start | bytes 3225608 | tf_op jit(solution)/shard_map/ppermute | solution.py:59
  4.4 2.4 collective-permute-start
  6.8 23.2 %collective-permute-done.1 = bf16[4,600,224]{1,2,0:T(8,128)(2,1)S(1)} collective-permute-done((bf16[4,600,224]{1,2,0:T(8,128)(2,1)}, bf16[4,600,224]{1,2,0:T(8,128)(2,1)S(1)}, u32[]{:S(2)}, u32[]{:S(2)}) %collective-permute-start.1) | collective-permute-done | bytes 1075232 | tf_op jit(solution)/shard_map/ppermute | solution.py:59
  31.0 4.5 %collective-permute-start.2 = (bf16[4,600,224]{1,2,0:T(8,128)(2,1)S(1)}, bf16[4,600,224]{1,2,0:T(8,128)(2,1)}, u32[]{:S(2)}, u32[]{:S(2)}) collective-permute-start(bf16[4,600,224]{1,2,0:T(8,128)(2,1)S(1)} %collective-permute-done.1), channel_id=1, source_target_pairs={{4,8},{8,12},{5,9},{9,13},{6,10},{10,14},{7,11},{11,15},{20,24},{2... | collective-permute-start | bytes 3225608 | tf_op jit(solution)/shard_map/ppermute | solution.py:59
  35.5 1.9 collective-permute-start.4
  37.4 20.8 %collective-permute-done.2 = bf16[4,600,224]{1,2,0:T(8,128)(2,1)} collective-permute-done((bf16[4,600,224]{1,2,0:T(8,128)(2,1)S(1)}, bf16[4,600,224]{1,2,0:T(8,128)(2,1)}, u32[]{:S(2)}, u32[]{:S(2)}) %collective-permute-start.2) | collective-permute-done | bytes 1075232 | tf_op jit(solution)/shard_map/ppermute | solution.py:59
  58.2 1.7 collective-permute-start.3
  59.9 4.3 %all-to-all-start = ((bf16[4,600,224]{1,2,0:T(8,128)(2,1)}), bf16[4,600,224]{1,2,0:T(8,128)(2,1)}, u32[]{:S(2)}, u32[]{:S(2)}) async-start(bf16[4,600,224]{1,2,0:T(8,128)(2,1)} %param.11), calls=%async_computation | async-start | bytes 2293760 | tf_op jit(solution)/shard_map/all_to_all | solution.py:166
  64.2 1.9 slice.6
  66.2 2.4 slice.7
  68.6 2.7 copy.45
  71.3 1.8 copy.46
  73.1 1.4 collective-permute-start.5
  74.5 3.4 %fusion.67 = f32[16,10]{1,0:T(8,128)S(1)} fusion(f32[16,10]{1,0:T(8,128)S(1)} %broadcast_in_dim.16, s32[]{:T(128)S(6)} %select_n.85, bf16[10,600,224]{1,2,0:T(8,128)(2,1)S(1)} %copy-done, bf16[4,600,224]{1,2,0:T(8,128)(2,1)} %param.6), kind=kOutput, calls=%fused_computation.51 | convolution fusion | flops 10752000 | bytes 3944452 | tf_op jit(solution)/shard_map/wiq,giq->wg/dot_general | solution.py:86
  78.0 2.1 copy.30
  81.3 1.9 add.110
  83.2 1.9 add.106
  85.2 2.0 fusion.77
  87.2 12.9 %collective-permute-done.5 = bf16[4,600,224]{1,2,0:T(8,128)(2,1)S(1)} collective-permute-done((bf16[4,600,224]{1,2,0:T(8,128)(2,1)}, bf16[4,600,224]{1,2,0:T(8,128)(2,1)S(1)}, u32[]{:S(2)}, u32[]{:S(2)}) %collective-permute-start.5) | collective-permute-done | bytes 1075232 | tf_op jit(solution)/shard_map/ppermute | solution.py:59
  100.4 2.0 fusion.87
  102.4 2.0 fusion.97
  104.4 7.1 %psum.7 = f32[16,10]{1,0:T(8,128)S(1)} all-reduce(f32[16,10]{1,0:T(8,128)S(1)} %fusion.97), channel_id=1, replica_groups=mesh['grp'=2,'chol'=4,'orb'=4] {'orb'}, use_global_device_ids=true, to_apply=%region_0.1 | all-reduce | flops 160 | bytes 1280 | tf_op jit(solution)/shard_map/psum | solution.py:88
  112.8 1.7 collective-permute-start.6
  114.5 2.5 fusion.58
  119.7 20.9 %collective-permute-done.6 = bf16[16,10]{1,0:T(8,128)(2,1)S(1)} collective-permute-done((bf16[16,10]{1,0:T(8,128)(2,1)S(1)}, bf16[16,10]{1,0:T(8,128)(2,1)S(1)}, u32[]{:S(2)}, u32[]{:S(2)}) %collective-permute-start.6) | collective-permute-done | bytes 352 | tf_op jit(solution)/shard_map/ppermute | solution.py:59
  140.6 2.7 add_convert_fusion.1
  143.4 6.6 %collective-permute-start.9 = (bf16[4,144,896]{2,0,1:T(4,128)(2,1)S(1)}, bf16[4,144,896]{2,0,1:T(4,128)(2,1)S(1)}, u32[]{:S(2)}, u32[]{:S(2)}) collective-permute-start(bf16[4,144,896]{2,0,1:T(4,128)(2,1)S(1)} %add_convert_fusion.1), channel_id=1, source_target_pairs={{4,8},{8,4},{5,9},{9,5},{6,10},{10,6},{7,11},{11,7},{20,24},{24,20... | collective-permute-start | bytes 3096584 | tf_op jit(solution)/shard_map/ppermute | solution.py:59
  152.8 2.7 add_convert_fusion.3
  155.6 1.9 collective-permute-start.8
  157.5 16.1 %collective-permute-done.9 = bf16[4,144,896]{2,0,1:T(4,128)(2,1)S(1)} collective-permute-done((bf16[4,144,896]{2,0,1:T(4,128)(2,1)S(1)}, bf16[4,144,896]{2,0,1:T(4,128)(2,1)S(1)}, u32[]{:S(2)}, u32[]{:S(2)}) %collective-permute-start.9) | collective-permute-done | bytes 1032224 | tf_op jit(solution)/shard_map/ppermute | solution.py:59
  173.6 3.0 %add_convert_fusion = bf16[4,144,896]{2,0,1:T(4,128)(2,1)S(1)} fusion(f32[4,144,896]{2,0,1:T(4,128)S(1)} %fusion.54, bf16[4,144,896]{2,0,1:T(4,128)(2,1)S(1)} %collective-permute-done.9, bf16[10,144,896]{2,1,0:T(8,128)(2,1)} %collective-permute-done.7, bf16[16,10]{1,0:T(8,128)(2,1)S(1)} %collective-permute-done.6, s32[]{:T(128)S(6)} %select_n.99), kind=kOutput, calls=%fused_computation.25 | convolution fusion | flops 12386304 | bytes 6710276 | tf_op jit(solution)/shard_map/wg,gpq->wpq/dot_general | solution.py:51
  176.6 1.4 collective-permute-start.10
  178.0 6.9 %collective-permute-done.11 = bf16[10,80,896]{2,1,0:T(8,128)(2,1)S(1)} collective-permute-done((bf16[10,80,896]{2,1,0:T(8,128)(2,1)S(1)}, bf16[10,80,896]{2,1,0:T(8,128)(2,1)S(1)}, u32[]{:S(2)}, u32[]{:S(2)}) %collective-permute-start.11) | collective-permute-done | bytes 1433632 | tf_op jit(solution)/shard_map/ppermute | solution.py:59
  185.4 2.2 collective-permute-start.13
  188.7 3.6 %collective-permute-start.12 = (bf16[4,80,896]{2,0,1:T(4,128)(2,1)S(1)}, bf16[4,80,896]{2,0,1:T(4,128)(2,1)}, u32[]{:S(2)}, u32[]{:S(2)}) collective-permute-start(bf16[4,80,896]{2,0,1:T(4,128)(2,1)S(1)} %fusion.47), channel_id=1, source_target_pairs={{4,8},{8,4},{5,9},{9,5},{6,10},{10,6},{7,11},{11,7},{20,24},{24,20... | collective-permute-start | bytes 1720328 | tf_op jit(solution)/shard_map/ppermute | solution.py:59
  192.4 15.6 %collective-permute-done.13 = bf16[4,80,896]{2,0,1:T(4,128)(2,1)S(1)} collective-permute-done((bf16[4,80,896]{2,0,1:T(4,128)(2,1)S(1)}, bf16[4,80,896]{2,0,1:T(4,128)(2,1)S(1)}, u32[]{:S(2)}, u32[]{:S(2)}) %collective-permute-start.13) | collective-permute-done | bytes 573472 | tf_op jit(solution)/shard_map/ppermute | solution.py:59
  208.0 1.5 add_convert_fusion.4
  209.6 2.1 collective-permute-start.14
  211.7 3.3 %broadcast_select_fusion = bf16[4,144,896]{2,0,1:T(4,128)(2,1)S(1)} fusion(bf16[4,144,896]{2,0,1:T(4,128)(2,1)S(1)} %collective-permute-done.10, pred[]{:T(512)S(6)} %and.26, f32[4,144,896]{2,0,1:T(4,128)S(1)} %fusion.58, bf16[10,144,896]{2,1,0:T(8,128)(2,1)} %collective-permute-done.7, bf16[4,144,896]{2,0,1:T(4,128)(2,1)S(1)} %collective-permute-done.8, ...), kind=kOutput, calls=%fused_computation.58 | convolution fusion | flops 12902400 | bytes 7742469 | tf_op jit(solution)/shard_map/wg,gpq->wpq/dot_general | solution.py:51
  216.1 4.2 %all-to-all-start.1 = ((bf16[4,144,896]{2,1,0:T(8,128)(2,1)}), bf16[4,144,896]{2,1,0:T(8,128)(2,1)}, u32[]{:S(2)}, u32[]{:S(2)}) async-start(bf16[4,144,896]{2,1,0:T(8,128)(2,1)} %copy.35), calls=%async_computation.1 | async-start | bytes 2064384 | tf_op jit(solution)/shard_map/all_to_all | solution.py:182
  222.3 1.5 fusion.112
  224.6 10.0 %all-to-all-done.1 = bf16[4,144,896]{2,1,0:T(8,128)(2,1)} async-done(((bf16[4,144,896]{2,1,0:T(8,128)(2,1)}), bf16[4,144,896]{2,1,0:T(8,128)(2,1)}, u32[]{:S(2)}, u32[]{:S(2)}) %all-to-all-start.1) | async-done | bytes 1032224 | tf_op jit(solution)/shard_map/all_to_all | solution.py:182
  234.7 3.5 %all-to-all-start.2 = ((bf16[4,80,896]{2,1,0:T(8,128)(2,1)}), bf16[4,80,896]{2,1,0:T(8,128)(2,1)S(1)}, u32[]{:S(2)}, u32[]{:S(2)}) async-start(bf16[4,80,896]{2,1,0:T(8,128)(2,1)} %copy.42), calls=%async_computation.2 | async-start | bytes 1146880 | tf_op jit(solution)/shard_map/all_to_all | solution.py:182
  238.1 1.6 copy.43.held_ref
  239.7 7.8 %all-to-all-done.2 = bf16[4,80,896]{2,1,0:T(8,128)(2,1)S(1)} async-done(((bf16[4,80,896]{2,1,0:T(8,128)(2,1)}), bf16[4,80,896]{2,1,0:T(8,128)(2,1)S(1)}, u32[]{:S(2)}, u32[]{:S(2)}) %all-to-all-start.2) | async-done | bytes 573472 | tf_op jit(solution)/shard_map/all_to_all | solution.py:182
  248.8 8.1 %shard_map.77 = bf16[4,600,224]{2,1,0:T(8,128)(2,1)S(1)} custom-call(bf16[4,600,224]{2,1,0:T(8,128)(2,1)S(1)} %copy.43.held_ref, bf16[896,896]{1,0:T(8,128)(2,1)S(1)} %bitcast.51), custom_call_target="tpu_custom_call" | custom-call | flops 5780275200 | bytes 3225600 | tf_op jit(solution)/shard_map/pallas_call | solution.py:143
  258.0 2.5 copy.44
  260.5 19.0 %all_to_all.20 = bf16[4,600,224]{1,2,0:T(8,128)(2,1)S(1)} all-to-all(bf16[4,600,224]{1,2,0:T(8,128)(2,1)} %copy.44), channel_id=1, replica_groups=mesh['grp'=2,'chol'=4,'orb'=4] {'orb'}, dimensions={0} | all-to-all | bytes 2150400 | tf_op jit(solution)/shard_map/all_to_all | solution.py:187
  (65 shorter events, 18.3 us)
Async XLA Ops:
  0.6 73.9 %copy-start = (bf16[10,600,224]{1,2,0:T(8,128)(2,1)S(1)}, bf16[10,600,224]{1,2,0:T(8,128)(2,1)}, u32[]{:S(2)}) copy-start(bf16[10,600,224]{1,2,0:T(8,128)(2,1)} %param.7) | copy-start | bytes 8064004
  0.6 29.4 %collective-permute-start.1 = (bf16[4,600,224]{1,2,0:T(8,128)(2,1)}, bf16[4,600,224]{1,2,0:T(8,128)(2,1)S(1)}, u32[]{:S(2)}, u32[]{:S(2)}) collective-permute-start(bf16[4,600,224]{1,2,0:T(8,128)(2,1)} %param.6), channel_id=1, source_target_pairs={{0,4},{4,8},{8,12},{1,5},{5,9},{9,13},{2,6},{6,10},{10,14},{3,7},{... | collective-permute-start | bytes 3225608 | tf_op jit(solution)/shard_map/ppermute | solution.py:59
  4.4 31.1 %collective-permute-start = (bf16[4,600,224]{1,2,0:T(8,128)(2,1)}, bf16[4,600,224]{1,2,0:T(8,128)(2,1)}, u32[]{:S(2)}, u32[]{:S(2)}) collective-permute-start(bf16[4,600,224]{1,2,0:T(8,128)(2,1)} %param.6), channel_id=1, source_target_pairs={{4,0},{8,4},{12,8},{5,1},{9,5},{13,9},{6,2},{10,6},{14,10},{7,3},{... | collective-permute-start | bytes 3225608 | tf_op jit(solution)/shard_map/ppermute | solution.py:59
  30.0 1.0 copy-start.12
  31.0 27.2 %collective-permute-start.2 = (bf16[4,600,224]{1,2,0:T(8,128)(2,1)S(1)}, bf16[4,600,224]{1,2,0:T(8,128)(2,1)}, u32[]{:S(2)}, u32[]{:S(2)}) collective-permute-start(bf16[4,600,224]{1,2,0:T(8,128)(2,1)S(1)} %collective-permute-done.1), channel_id=1, source_target_pairs={{4,8},{8,12},{5,9},{9,13},{6,10},{10,14},{7,11},{11,15},{20,24},{2... | collective-permute-start | bytes 3225608 | tf_op jit(solution)/shard_map/ppermute | solution.py:59
  35.5 37.6 %collective-permute-start.4 = (bf16[4,600,224]{1,2,0:T(8,128)(2,1)}, bf16[4,600,224]{1,2,0:T(8,128)(2,1)}, u32[]{:S(2)}, u32[]{:S(2)}) collective-permute-start(bf16[4,600,224]{1,2,0:T(8,128)(2,1)} %collective-permute-done), channel_id=1, source_target_pairs={{8,4},{4,0},{9,5},{5,1},{10,6},{6,2},{11,7},{7,3},{24,20},{20,16},... | collective-permute-start | bytes 3225608 | tf_op jit(solution)/shard_map/ppermute | solution.py:59
  58.2 25.0 %collective-permute-start.3 = (bf16[4,600,224]{1,2,0:T(8,128)(2,1)}, bf16[4,600,224]{1,2,0:T(8,128)(2,1)}, u32[]{:S(2)}, u32[]{:S(2)}) collective-permute-start(bf16[4,600,224]{1,2,0:T(8,128)(2,1)} %collective-permute-done.2), channel_id=1, source_target_pairs={{8,12},{9,13},{10,14},{11,15},{24,28},{25,29},{26,30},{27,31}} | collective-permute-start | bytes 3225608 | tf_op jit(solution)/shard_map/ppermute | solution.py:59
  59.9 156.2 %all-to-all-start = ((bf16[4,600,224]{1,2,0:T(8,128)(2,1)}), bf16[4,600,224]{1,2,0:T(8,128)(2,1)}, u32[]{:S(2)}, u32[]{:S(2)}) async-start(bf16[4,600,224]{1,2,0:T(8,128)(2,1)} %param.11), calls=%async_computation | async-start | bytes 2293760 | tf_op jit(solution)/shard_map/all_to_all | solution.py:166
  66.2 5.1 %copy-start.3 = (bf16[10,144,896]{2,1,0:T(8,128)(2,1)}, bf16[10,144,896]{2,1,0:T(8,128)(2,1)S(1)}, u32[]{:S(2)}) copy-start(bf16[10,144,896]{2,1,0:T(8,128)(2,1)S(1)} %slice.6) | copy-start | bytes 7741444
  68.6 2.7 copy-start.5
  71.3 1.8 copy-start.15
  73.1 27.0 %collective-permute-start.5 = (bf16[4,600,224]{1,2,0:T(8,128)(2,1)}, bf16[4,600,224]{1,2,0:T(8,128)(2,1)S(1)}, u32[]{:S(2)}, u32[]{:S(2)}) collective-permute-start(bf16[4,600,224]{1,2,0:T(8,128)(2,1)} %collective-permute-done.4), channel_id=1, source_target_pairs={{4,0},{5,1},{6,2},{7,3},{20,16},{21,17},{22,18},{23,19}} | collective-permute-start | bytes 3225608 | tf_op jit(solution)/shard_map/ppermute | solution.py:59
  74.5 3.4 %copy-start.10 = (bf16[10,144,896]{2,0,1:T(8,128)(2,1)S(1)}, bf16[10,144,896]{2,0,1:T(8,128)(2,1)}, u32[]{:S(2)}) copy-start(bf16[10,144,896]{2,0,1:T(8,128)(2,1)} %copy.45) | copy-start | bytes 7741444
  80.1 60.6 %collective-permute-start.7 = (bf16[10,144,896]{2,1,0:T(8,128)(2,1)}, bf16[10,144,896]{2,1,0:T(8,128)(2,1)}, u32[]{:S(2)}, u32[]{:S(2)}) collective-permute-start(bf16[10,144,896]{2,1,0:T(8,128)(2,1)} %copy.30), channel_id=1, source_target_pairs={{0,4},{12,8},{1,5},{13,9},{2,6},{14,10},{3,7},{15,11},{16,20},{28,... | collective-permute-start | bytes 7741448 | tf_op jit(solution)/shard_map/ppermute | solution.py:59
  85.1 14.9 %copy-start.13 = (bf16[4,600,224]{1,2,0:T(8,128)(2,1)S(1)}, bf16[4,600,224]{1,2,0:T(8,128)(2,1)}, u32[]{:S(2)}) copy-start(bf16[4,600,224]{1,2,0:T(8,128)(2,1)} %copy-done.12) | copy-start | bytes 3225604
  102.4 9.7 %copy-start.14 = (f32[16,10]{1,0:T(8,128)S(1)}, f32[16,10]{1,0:T(8,128)}, u32[]{:S(2)}) copy-start(f32[16,10]{1,0:T(8,128)} %param.9) | copy-start | bytes 1924
  112.8 4.3 %copy-start.4 = (bf16[10,144,896]{2,1,0:T(8,128)(2,1)S(1)}, bf16[10,144,896]{2,1,0:T(8,128)(2,1)}, u32[]{:S(2)}) copy-start(bf16[10,144,896]{2,1,0:T(8,128)(2,1)} %copy-done.3) | copy-start | bytes 7741444
  112.8 27.9 %collective-permute-start.6 = (bf16[16,10]{1,0:T(8,128)(2,1)S(1)}, bf16[16,10]{1,0:T(8,128)(2,1)S(1)}, u32[]{:S(2)}, u32[]{:S(2)}) collective-permute-start(bf16[16,10]{1,0:T(8,128)(2,1)S(1)} %get-tuple-element.8), channel_id=1, source_target_pairs={{0,4},{12,8},{1,5},{13,9},{2,6},{14,10},{3,7},{15,11},{16,20},{28,... | collective-permute-start | bytes 968 | tf_op jit(solution)/shard_map/ppermute | solution.py:59
  117.8 1.4 copy-start.6
  119.7 30.3 %copy-start.11 = (bf16[10,80,896]{2,0,1:T(8,128)(2,1)S(1)}, bf16[10,80,896]{2,0,1:T(8,128)(2,1)}, u32[]{:S(2)}) copy-start(bf16[10,80,896]{2,0,1:T(8,128)(2,1)} %copy.46) | copy-start | bytes 4300804
  143.4 30.2 %collective-permute-start.9 = (bf16[4,144,896]{2,0,1:T(4,128)(2,1)S(1)}, bf16[4,144,896]{2,0,1:T(4,128)(2,1)S(1)}, u32[]{:S(2)}, u32[]{:S(2)}) collective-permute-start(bf16[4,144,896]{2,0,1:T(4,128)(2,1)S(1)} %add_convert_fusion.1), channel_id=1, source_target_pairs={{4,8},{8,4},{5,9},{9,5},{6,10},{10,6},{7,11},{11,7},{20,24},{24,20... | collective-permute-start | bytes 3096584 | tf_op jit(solution)/shard_map/ppermute | solution.py:59
  150.2 34.6 %collective-permute-start.11 = (bf16[10,80,896]{2,1,0:T(8,128)(2,1)S(1)}, bf16[10,80,896]{2,1,0:T(8,128)(2,1)S(1)}, u32[]{:S(2)}, u32[]{:S(2)}) collective-permute-start(bf16[10,80,896]{2,1,0:T(8,128)(2,1)S(1)} %copy.37), channel_id=1, source_target_pairs={{0,4},{12,8},{1,5},{13,9},{2,6},{14,10},{3,7},{15,11},{16,20},{28,... | collective-permute-start | bytes 4300808 | tf_op jit(solution)/shard_map/ppermute | solution.py:59
  155.6 56.1 %collective-permute-start.8 = (bf16[4,144,896]{2,0,1:T(4,128)(2,1)S(1)}, bf16[4,144,896]{2,0,1:T(4,128)(2,1)S(1)}, u32[]{:S(2)}, u32[]{:S(2)}) collective-permute-start(bf16[4,144,896]{2,0,1:T(4,128)(2,1)S(1)} %add_convert_fusion.3), channel_id=1, source_target_pairs={{4,8},{8,4},{5,9},{9,5},{6,10},{10,6},{7,11},{11,7},{20,24},{24,20... | collective-permute-start | bytes 3096584 | tf_op jit(solution)/shard_map/ppermute | solution.py:59
  176.6 35.0 %collective-permute-start.10 = (bf16[4,144,896]{2,0,1:T(4,128)(2,1)S(1)}, bf16[4,144,896]{2,0,1:T(4,128)(2,1)S(1)}, u32[]{:S(2)}, u32[]{:S(2)}) collective-permute-start(bf16[4,144,896]{2,0,1:T(4,128)(2,1)S(1)} %add_convert_fusion), channel_id=1, source_target_pairs={{4,0},{8,12},{5,1},{9,13},{6,2},{10,14},{7,3},{11,15},{20,16},{24,... | collective-permute-start | bytes 3096584 | tf_op jit(solution)/shard_map/ppermute | solution.py:59
  184.9 23.2 %copy-start.8 = (bf16[10,80,896]{2,1,0:T(8,128)(2,1)}, bf16[10,80,896]{2,1,0:T(8,128)(2,1)S(1)}, u32[]{:S(2)}) copy-start(bf16[10,80,896]{2,1,0:T(8,128)(2,1)S(1)} %collective-permute-done.11) | copy-start | bytes 4300804
  185.4 22.6 %collective-permute-start.13 = (bf16[4,80,896]{2,0,1:T(4,128)(2,1)S(1)}, bf16[4,80,896]{2,0,1:T(4,128)(2,1)S(1)}, u32[]{:S(2)}, u32[]{:S(2)}) collective-permute-start(bf16[4,80,896]{2,0,1:T(4,128)(2,1)S(1)} %fusion.44), channel_id=1, source_target_pairs={{4,8},{8,4},{5,9},{9,5},{6,10},{10,6},{7,11},{11,7},{20,24},{24,20... | collective-permute-start | bytes 1720328 | tf_op jit(solution)/shard_map/ppermute | solution.py:59
  188.7 33.5 %collective-permute-start.12 = (bf16[4,80,896]{2,0,1:T(4,128)(2,1)S(1)}, bf16[4,80,896]{2,0,1:T(4,128)(2,1)}, u32[]{:S(2)}, u32[]{:S(2)}) collective-permute-start(bf16[4,80,896]{2,0,1:T(4,128)(2,1)S(1)} %fusion.47), channel_id=1, source_target_pairs={{4,8},{8,4},{5,9},{9,5},{6,10},{10,6},{7,11},{11,7},{20,24},{24,20... | collective-permute-start | bytes 1720328 | tf_op jit(solution)/shard_map/ppermute | solution.py:59
  209.6 12.7 %collective-permute-start.14 = (bf16[4,80,896]{2,0,1:T(4,128)(2,1)}, bf16[4,80,896]{2,0,1:T(4,128)(2,1)}, u32[]{:S(2)}, u32[]{:S(2)}) collective-permute-start(bf16[4,80,896]{2,0,1:T(4,128)(2,1)} %add_convert_fusion.4), channel_id=1, source_target_pairs={{4,0},{8,12},{5,1},{9,13},{6,2},{10,14},{7,3},{11,15},{20,16},{24,... | collective-permute-start | bytes 1720328 | tf_op jit(solution)/shard_map/ppermute | solution.py:59
  215.0 5.3 %copy-start.7 = (bf16[10,80,896]{2,1,0:T(8,128)(2,1)S(1)}, bf16[10,80,896]{2,1,0:T(8,128)(2,1)}, u32[]{:S(2)}) copy-start(bf16[10,80,896]{2,1,0:T(8,128)(2,1)} %copy-done.5) | copy-start | bytes 4300804
  216.1 18.6 %all-to-all-start.1 = ((bf16[4,144,896]{2,1,0:T(8,128)(2,1)}), bf16[4,144,896]{2,1,0:T(8,128)(2,1)}, u32[]{:S(2)}, u32[]{:S(2)}) async-start(bf16[4,144,896]{2,1,0:T(8,128)(2,1)} %copy.35), calls=%async_computation.1 | async-start | bytes 2064384 | tf_op jit(solution)/shard_map/all_to_all | solution.py:182
  220.3 1.4 copy-start.9
  234.7 12.8 %all-to-all-start.2 = ((bf16[4,80,896]{2,1,0:T(8,128)(2,1)}), bf16[4,80,896]{2,1,0:T(8,128)(2,1)S(1)}, u32[]{:S(2)}, u32[]{:S(2)}) async-start(bf16[4,80,896]{2,1,0:T(8,128)(2,1)} %copy.42), calls=%async_computation.2 | async-start | bytes 1146880 | tf_op jit(solution)/shard_map/all_to_all | solution.py:182
  256.9 1.1 copy-start.2
  258.0 22.5 %copy-start.1 = (bf16[10,600,224]{1,2,0:T(8,128)(2,1)S(1)}, bf16[10,600,224]{1,2,0:T(8,128)(2,1)}, u32[]{:S(2)}) copy-start(bf16[10,600,224]{1,2,0:T(8,128)(2,1)} %param.7) | copy-start | bytes 8064004
